TPU v7x, 32 devices: a whole 2x2x4 slice. The times are simulated.
32 devices in a mesh: groups: 2 (over x), blk: 8 (over z, y), tensor: 2 (over core).
Axes of the slice: x: 2, y: 2, z: 4, core: 2. Of those that a mesh axis runs over, the one named last changes fastest.
Arguments:
- queries: bfloat16 [2048, 8192], P(('groups', 'blk'), 'tensor'), parts along dimension 0, may hold values from -64 to 64
- new_keys: bfloat16 [2048, 1024], P(('groups', 'blk'), 'tensor'), parts along dimension 0, may hold values from -24 to 24
- new_values: bfloat16 [2048, 1024], P(('groups', 'blk'), 'tensor'), parts along dimension 0, may hold values from -6 to 6
- prefix_keys: bfloat16 [2048, 1024], P(('groups', 'blk'), 'tensor'), parts along dimension 0, may hold values from -24 to 24
- prefix_values: bfloat16 [2048, 1024], P(('groups', 'blk'), 'tensor'), parts along dimension 0, may hold values from -6 to 6
- span_lens: int32 [4], P('groups'), parts along dimension 0, may hold values from 1 to 768, 1024 in all
- prefix_lens: int32 [4], P('groups'), parts along dimension 0, may hold values from 1 to 640, 1024 in all
- placement: int32 [2048], P('groups'), parts along dimension 0, may hold values from 0 to 1023, as said below
- decode_dest: int32 [2048, 1], P('groups'), parts along dimension 0, may hold values from 0 to 7; in each aligned block of 128 rows (0 to 127, 128 to 255, ...) at most 32 rows name the same one
Outputs:
- attended: bfloat16 [2048, 8192], P(('groups', 'blk'), 'tensor'), parts along dimension 0
- decode_keys: bfloat16 [4096, 1024], P(('groups', 'blk'), 'tensor'), parts along dimension 0
- decode_values: bfloat16 [4096, 1024], P(('groups', 'blk'), 'tensor'), parts along dimension 0
There are 2 independent parts, one for each index of `groups`. A program takes and returns all parts, laid end to end along the dimension named above; each array names one. Nothing has to cross between parts.
Inputs may be any that keep to these rules, and one draw needn't show every extreme that they name: `placement`: each aligned run of 64 slots holds 64 consecutive tokens in rising order; every token has exactly one slot. `decode_dest`: among the 128 slots of one cycle instance at most 32 go to any one decode instance, and in every draw some instance sends exactly 32 to some decode instance.
All inputs are finite; a program needn't handle non-finite values.
Results may differ from a plain program's by a relative error of at most 0.006.
Values may be sent and summed in bfloat16 or wider, within the bound.
No kernel may reach another device: no remote copies, remote signals or barrier semaphores. Data moves between devices by JAX's collectives and lax.ppermute only.
A program may use at most 128 MiB of HBM per device.

v0:
```python
import math

import jax
import jax.numpy as jnp
from jax import lax
from jax.sharding import PartitionSpec as P

H = 64
KVH = 8
HD = 128


masked_score = -1e30


def request_of(index, lens):
    ends = jnp.cumsum(lens)
    return jnp.sum((index[:, None] >= ends[None, :]).astype(jnp.int32), axis=1)


def block_rows_for(length):
    chosen = 512
    while length % chosen:
        chosen = chosen // 2
    return chosen


def attend(carried, query_groups, query_req, query_tok, keys, values, key_req, key_tok):
    length = keys.shape[0]
    chosen = block_rows_for(length)
    blocks = length // chosen
    heads_here = query_groups.shape[1]
    score_scale = 1.0 / math.sqrt(HD)
    key_blocks = keys.reshape(blocks, chosen, heads_here, HD)
    value_blocks = values.reshape(blocks, chosen, heads_here, HD)
    req_blocks = key_req.reshape(blocks, chosen)
    tok_blocks = key_tok.reshape(blocks, chosen)

    def one_block(inner, items):
        running_max, running_sum, numerator = inner
        key_part, value_part, req_part, tok_part = items
        visible = (req_part[None, :] == query_req[:, None]) & (
            tok_part[None, :] <= query_tok[:, None]
        )
        scores = (
            jnp.einsum("tkgd,nkd->kgtn", query_groups, key_part, preferred_element_type=jnp.float32)
            * score_scale
        )
        scores = jnp.where(visible, scores, masked_score)
        new_max = jnp.maximum(running_max, jnp.max(scores, axis=-1))
        rescale = jnp.exp(running_max - new_max)
        weights = jnp.where(visible, jnp.exp(scores - new_max[..., None]), 0.0)
        running_sum = running_sum * rescale + jnp.sum(weights, axis=-1)
        numerator = numerator * rescale[..., None] + jnp.einsum(
            "kgtn,nkd->kgtd",
            weights.astype(jnp.bfloat16),
            value_part,
            preferred_element_type=jnp.float32,
        )
        return ((new_max, running_sum, numerator), None)

    result, ignored = lax.scan(
        one_block, carried, (key_blocks, value_blocks, req_blocks, tok_blocks)
    )
    return result


def maybe_attend(
    carried, query_groups, query_req, query_tok, summary, keys, values, key_req, key_tok
):
    query_has, query_last = summary
    request_ids = jnp.arange(query_has.shape[0], dtype=jnp.int32)
    matches = key_req[:, None] == request_ids[None, :]
    wanted = jnp.any(matches & query_has[None, :], axis=1)
    latest = jnp.max(jnp.where(matches, query_last[None, :], -2), axis=1)
    touched = jnp.any(wanted & (key_tok <= latest))
    return lax.cond(
        touched,
        lambda inner: attend(
            inner, query_groups, query_req, query_tok, keys, values, key_req, key_tok
        ),
        lambda inner: inner,
        carried,
    )


def shards(
    queries,
    new_keys,
    new_values,
    prefix_keys,
    prefix_values,
    span_lens,
    prefix_lens,
    placement,
    decode_dest,
):
    cycle_size = lax.axis_size("blk")
    my_index = lax.axis_index("blk")
    rows_here = queries.shape[0]
    kv_cols = new_keys.shape[1]
    heads_here = kv_cols // HD
    groups = H // KVH
    query_groups = queries.reshape(rows_here, heads_here, groups, HD)
    query_tok = lax.dynamic_slice_in_dim(placement, my_index * rows_here, rows_here)
    query_req = request_of(query_tok, span_lens)
    token_req = request_of(placement, span_lens)
    prefix_total = prefix_keys.shape[0] * cycle_size
    prefix_req = request_of(jnp.arange(prefix_total, dtype=jnp.int32), prefix_lens)
    request_ids = jnp.arange(span_lens.shape[0], dtype=jnp.int32)
    member = query_req[:, None] == request_ids[None, :]
    summary = (jnp.any(member, axis=0), jnp.max(jnp.where(member, query_tok[:, None], -1), axis=0))
    initial = (
        jnp.full((heads_here, groups, rows_here), masked_score, jnp.float32),
        jnp.zeros((heads_here, groups, rows_here), jnp.float32),
        jnp.zeros((heads_here, groups, rows_here, HD), jnp.float32),
    )
    piece_keys = lax.all_gather(prefix_keys, "blk", axis=0, tiled=True)
    piece_values = lax.all_gather(prefix_values, "blk", axis=0, tiled=True)
    length = piece_keys.shape[0]
    key_req = prefix_req
    key_tok = jnp.full((length,), -1, jnp.int32)
    carried = maybe_attend(
        initial,
        query_groups,
        query_req,
        query_tok,
        summary,
        piece_keys,
        piece_values,
        key_req,
        key_tok,
    )
    destination = decode_dest[:, 0]
    capacity = 2 * rows_here // cycle_size
    piece_keys = lax.all_gather(new_keys, "blk", axis=0, tiled=True)
    piece_values = lax.all_gather(new_values, "blk", axis=0, tiled=True)
    key_req = token_req
    key_tok = placement
    carried = maybe_attend(
        carried,
        query_groups,
        query_req,
        query_tok,
        summary,
        piece_keys,
        piece_values,
        key_req,
        key_tok,
    )
    local_dest = lax.dynamic_slice_in_dim(destination, my_index * rows_here, rows_here)
    one_hot = (local_dest[:, None] == jnp.arange(cycle_size, dtype=jnp.int32)[None, :]).astype(
        jnp.int32
    )
    slot_rank = jnp.sum(jnp.cumsum(one_hot, axis=0) * one_hot, axis=1) - 1
    target = local_dest * capacity + slot_rank
    selector = (
        jnp.arange(cycle_size * capacity, dtype=jnp.int32)[:, None] == target[None, :]
    ).astype(jnp.bfloat16)
    stacked = jnp.concatenate([new_keys, new_values], axis=1)
    outgoing = jnp.dot(selector, stacked, preferred_element_type=jnp.float32).astype(jnp.bfloat16)
    moved = lax.all_to_all(outgoing, "blk", split_axis=0, concat_axis=0, tiled=True)
    running_max, running_sum, numerator = carried
    attended = (
        (numerator / running_sum[..., None])
        .transpose(2, 0, 1, 3)
        .reshape(rows_here, heads_here * groups * HD)
        .astype(jnp.bfloat16)
    )
    return (attended, moved[:, :kv_cols], moved[:, kv_cols:])


def solution(mesh):
    placed = (
        P(("groups", "blk"), "tensor"),
        P(("groups", "blk"), "tensor"),
        P(("groups", "blk"), "tensor"),
        P(("groups", "blk"), "tensor"),
        P(("groups", "blk"), "tensor"),
        P("groups"),
        P("groups"),
        P("groups"),
        P("groups", None),
    )
    return jax.shard_map(
        shards,
        mesh=mesh,
        in_specs=placed,
        out_specs=(
            P(("groups", "blk"), "tensor"),
            P(("groups", "blk"), "tensor"),
            P(("groups", "blk"), "tensor"),
        ),
        check_vma=False,
    )
```

profile of v0, /device:TPU:0, one launch (start us, length us, event | category | flops | bytes accessed | tf_op | source)
XLA Modules:
  0.0 219.7 jit_solution(14757538730293133213)
XLA Ops:
  7.2 0.7 all-gather.5.cloned.1.call-update
  7.9 0.7 all-gather.7.cloned.1.call-update
  8.7 0.7 all-gather.11.cloned.1.call-update
  11.7 2.0 convolution_convert_fusion
  13.8 7.3 %all-to-all-start = ((bf16[8,32,1024]{2,1,0:T(8,128)(2,1)}), bf16[8,32,1024]{2,1,0:T(8,128)(2,1)S(1)}, u32[]{:S(2)}, u32[]{:S(2)}) async-start(bf16[8,32,1024]{2,1,0:T(8,128)(2,1)} %bitcast.16), calls=%async_computation | async-start | bytes 1048576 | tf_op jit(solution)/shard_map/all_to_all | solution.py:162
  21.1 0.8 dynamic_slice.32
  21.8 0.8 reduce-window.16
  22.7 0.8 reduce-window.17
  23.9 0.8 fusion.32
  26.1 2.3 %copy.31 = bf16[128,4096]{0,1:T(8,128)(2,1)} copy(bf16[128,4096]{1,0:T(8,128)(2,1)} %param.17) | data formatting | bytes 2097152 | tf_op args[0]
  28.4 1.3 and_reduce_fusion.3
  30.4 9.4 %all-to-all-done = bf16[8,32,1024]{2,1,0:T(8,128)(2,1)S(1)} async-done(((bf16[8,32,1024]{2,1,0:T(8,128)(2,1)}), bf16[8,32,1024]{2,1,0:T(8,128)(2,1)S(1)}, u32[]{:S(2)}, u32[]{:S(2)}) %all-to-all-start) | async-done | bytes 524320 | tf_op jit(solution)/shard_map/all_to_all | solution.py:162
  39.8 0.8 fusion.37
  40.6 17.0 %all-gather.5.cloned.1.call-done = bf16[1024,512]{1,0:T(8,128)(2,1)} async-done(((bf16[128,512]{1,0:T(8,128)(2,1)}), bf16[1024,512]{1,0:T(8,128)(2,1)}) %all-gather.5.cloned.1.call-update) | async-done | bytes 1048592 | tf_op jit(solution)/shard_map/all_gather | solution.py:118
  57.5 41.1 %all-gather.7.cloned.1.call-done = bf16[1024,512]{1,0:T(8,128)(2,1)} async-done(((bf16[128,512]{1,0:T(8,128)(2,1)}), bf16[1024,512]{1,0:T(8,128)(2,1)}) %all-gather.7.cloned.1.call-update) | async-done | bytes 1048592 | tf_op jit(solution)/shard_map/all_gather | solution.py:119
  98.6 40.8 %conditional.2 = (f32[4,8,128]{2,1,0:T(8,128)}, f32[4,8,128]{2,1,0:T(8,128)}, f32[4,8,128,128]{3,2,1,0:T(8,128)}) conditional(s32[]{:T(128)} %convert_element_type.41, () %tuple.31, (bf16[1024,512]{1,0:T(8,128)(2,1)}, bf16[1024,512]{1,0:T(8,128)(2,1)}, s32[1024]{0:T(1024)S(1)}, s32[128]{0:T(128)S(1)}, s32[128]{0:T(128)S(1)}, ...), branch_computations={%region_13.14_spmd, %region_14.19_spmd} | conditional | flops 1102729344 | bytes 73940520 | solution.py:77
  98.6 1.6 copy.32
  100.2 1.3 reshape.98
  101.6 2.2 reshape.99
  103.8 35.6 %while.28 = (s32[]{:T(128)}, f32[4,8,128]{2,1,0:T(8,128)}, f32[4,8,128]{2,1,0:T(8,128)}, f32[4,8,128,128]{3,2,1,0:T(8,128)}, s32[2,512]{1,0:T(2,128)S(1)}, /*ind...) while((s32[]{:T(128)}, f32[4,8,128]{2,1,0:T(8,128)}, ...), condition=%wide.region_18.18_spmd.clone, body=%wide.region_15.17_spmd.clone.sunk | while | flops 1102729344 | bytes 67640744 | solution.py:62
  103.9 1.4 constant_dynamic-slice_fusion.14
  105.3 4.6 %fusion.56 = (f32[4,8,128]{2,1,0:T(8,128)S(1)}, f32[4,512,128,8]{2,1,3,0:T(8,128)}) fusion(pred[128,512]{0,1:T(8,128)(4,1)S(1)} %compare_and_fusion.5, bf16[128,4,8,128]{3,0,2,1:T(8,128)(2,1)S(1)} %get-tuple-element.570, bf16[1,512,4,128]{3,2,1,0:T(4,128)(2,1)S(1)} %get-tuple-element.496), kind=kOutput, calls=%fused_computation.23.clone.1 | convolution fusion | flops 543158272 | bytes 10043392 | tf_op jit(solution)/shard_map/cond/branch_1_fun/while/body/eval_jaxpr/tkgd,nkd->kgtn/dot_general | solution.py:46
  109.9 4.7 %fusion.57 = f32[4,8,128]{2,1,0:T(8,128)S(1)} fusion(f32[4,512,128,8]{2,1,3,0:T(8,128)} %get-tuple-element.498, f32[4,8,128]{2,1,0:T(8,128)S(1)} %select_maximum_fusion.2, pred[128,512]{0,1:T(8,128)(4,1)S(1)} %compare_and_fusion.5), kind=kLoop, calls=%fused_computation.25.clone.1 | loop fusion | flops 10481664 | bytes 8486912 | tf_op jit(solution)/shard_map/cond/branch_1_fun/while/body/eval_jaxpr/reduce_sum | solution.py:53
  115.8 4.1 %fusion.59 = f32[4,8,128,128]{3,2,1,0:T(8,128)} fusion(f32[4,8,128,128]{3,2,1,0:T(8,128)} %get-tuple-element.553, f32[4,512,128,8]{2,1,3,0:T(8,128)S(1)} %copy-done, f32[4,8,128]{2,1,0:T(8,128)S(1)} %select_maximum_fusion.2, pred[128,512]{0,1:T(8,128)(4,1)S(1)} %compare_and_fusion.5, f32[4,8,128]{2,1,0:T(8,128)S(1)} %get-tuple-element.500, ...), kind=kOutput, calls=%fused_computation.29.clone.1 | convolution fusion | flops 548929536 | bytes 13205505 | tf_op jit(solution)/shard_map/cond/branch_1_fun/while/body/eval_jaxpr/kgtn,nkd->kgtd/dot_general | solution.py:54
  120.6 1.4 constant_dynamic-slice_fusion.14
  122.0 4.6 %fusion.56 = (f32[4,8,128]{2,1,0:T(8,128)S(1)}, f32[4,512,128,8]{2,1,3,0:T(8,128)}) fusion(pred[128,512]{0,1:T(8,128)(4,1)S(1)} %compare_and_fusion.5, bf16[128,4,8,128]{3,0,2,1:T(8,128)(2,1)S(1)} %get-tuple-element.570, bf16[1,512,4,128]{3,2,1,0:T(4,128)(2,1)S(1)} %get-tuple-element.496), kind=kOutput, calls=%fused_computation.23.clone.1 | convolution fusion | flops 543158272 | bytes 10043392 | tf_op jit(solution)/shard_map/cond/branch_1_fun/while/body/eval_jaxpr/tkgd,nkd->kgtn/dot_general | solution.py:46
  126.6 0.9 select_maximum_fusion.2
  127.5 4.7 %fusion.57 = f32[4,8,128]{2,1,0:T(8,128)S(1)} fusion(f32[4,512,128,8]{2,1,3,0:T(8,128)} %get-tuple-element.498, f32[4,8,128]{2,1,0:T(8,128)S(1)} %select_maximum_fusion.2, pred[128,512]{0,1:T(8,128)(4,1)S(1)} %compare_and_fusion.5), kind=kLoop, calls=%fused_computation.25.clone.1 | loop fusion | flops 10481664 | bytes 8486912 | tf_op jit(solution)/shard_map/cond/branch_1_fun/while/body/eval_jaxpr/reduce_sum | solution.py:53
  132.2 1.4 fusion.58
  133.5 5.3 %fusion.59 = f32[4,8,128,128]{3,2,1,0:T(8,128)} fusion(f32[4,8,128,128]{3,2,1,0:T(8,128)} %get-tuple-element.553, f32[4,512,128,8]{2,1,3,0:T(8,128)S(1)} %copy-done, f32[4,8,128]{2,1,0:T(8,128)S(1)} %select_maximum_fusion.2, pred[128,512]{0,1:T(8,128)(4,1)S(1)} %compare_and_fusion.5, f32[4,8,128]{2,1,0:T(8,128)S(1)} %get-tuple-element.500, ...), kind=kOutput, calls=%fused_computation.29.clone.1 | convolution fusion | flops 548929536 | bytes 13205505 | tf_op jit(solution)/shard_map/cond/branch_1_fun/while/body/eval_jaxpr/kgtn,nkd->kgtd/dot_general | solution.py:54
  139.7 40.9 %all-gather.9.cloned.1.call-done = bf16[1024,512]{1,0:T(8,128)(2,1)} async-done(((bf16[128,512]{1,0:T(8,128)(2,1)}), bf16[1024,512]{1,0:T(8,128)(2,1)}) %all-gather.9.cloned.1.call-update) | async-done | bytes 1048592 | tf_op jit(solution)/shard_map/all_gather | solution.py:136
  180.7 28.5 %conditional.3 = ((f32[4,8,128]{2,1,0:T(8,128)}, f32[4,8,128,128]{3,2,1,0:T(8,128)})) conditional(s32[]{:T(128)} %convert_element_type.39, (f32[4,8,128]{2,1,0:T(8,128)}, f32[4,8,128,128]{3,2,1,0:T(8,128)}) %tuple.33, (bf16[1024,512]{1,0:T(8,128)(2,1)}, bf16[1024,512]{1,0:T(8,128)(2,1)}, s32[1024]{0:T(1024)S(1)}, s32[1024]{0:T(1024)S(1)}, ...), branch_computations={%region_19.20_spmd, %region_20.25_spmd} | conditional | flops 1102258176 | bytes 40400124 | solution.py:77
  180.7 1.6 copy.33
  182.3 1.3 reshape.102
  183.6 1.3 reshape.103
  185.0 24.1 %while.27 = (s32[]{:T(128)}, f32[4,8,128]{2,1,0:T(8,128)}, f32[4,8,128]{2,1,0:T(8,128)}, f32[4,8,128,128]{3,2,1,0:T(8,128)}, s32[2,512]{1,0:T(2,128)S(1)}, /*ind...) while((s32[]{:T(128)}, f32[4,8,128]{2,1,0:T(8,128)}, ...), condition=%wide.region_24.24_spmd, body=%wide.region_21.23_spmd.sunk | while | flops 1102258176 | bytes 34092156 | solution.py:62
  185.6 1.4 fusion.52
  187.0 0.7 max.10
  187.7 2.1 fusion.53
  189.8 1.3 multiply_add_fusion.4
  191.2 5.3 %multiply_add_fusion.5 = f32[4,8,128,128]{3,2,1,0:T(8,128)} fusion(f32[4,8,128,128]{3,2,1,0:T(8,128)} %get-tuple-element.517, f32[4,512,128,8]{2,1,3,0:T(8,128)S(1)} %get-tuple-element.482, f32[4,8,128]{2,1,0:T(8,128)S(1)} %max.10, pred[128,512]{0,1:T(8,128)(4,1)S(1)} %compare_and_fusion.4, f32[4,8,128]{2,1,0:T(8,128)S(1)} %get-tuple-element.484, ...), kind=kOutput, calls=%fused_computation.7.clone.1 | convolution fusion | flops 548405248 | bytes 13205504 | tf_op jit(solution)/shard_map/cond/branch_1_fun/while/body/eval_jaxpr/kgtn,nkd->kgtd/dot_general | solution.py:54
  197.7 1.4 fusion.52
  199.1 0.7 max.10
  199.8 2.1 fusion.53
  201.9 1.3 multiply_add_fusion.4
  203.2 5.3 %multiply_add_fusion.5 = f32[4,8,128,128]{3,2,1,0:T(8,128)} fusion(f32[4,8,128,128]{3,2,1,0:T(8,128)} %get-tuple-element.517, f32[4,512,128,8]{2,1,3,0:T(8,128)S(1)} %get-tuple-element.482, f32[4,8,128]{2,1,0:T(8,128)S(1)} %max.10, pred[128,512]{0,1:T(8,128)(4,1)S(1)} %compare_and_fusion.4, f32[4,8,128]{2,1,0:T(8,128)S(1)} %get-tuple-element.484, ...), kind=kOutput, calls=%fused_computation.7.clone.1 | convolution fusion | flops 548405248 | bytes 13205504 | tf_op jit(solution)/shard_map/cond/branch_1_fun/while/body/eval_jaxpr/kgtn,nkd->kgtd/dot_general | solution.py:54
  209.1 2.0 fusion.26
  211.8 1.4 copy.59
  (49 shorter events, 9.8 us)
Async XLA Ops:
  7.2 50.4 %all-gather.5.cloned.1.call-start = ((), (), s32[]{:S(2)}) async-start(), calls=%async_computation.1 | async-start | bytes 1179648 | tf_op jit(solution)/shard_map/all_gather | solution.py:118
  7.9 90.7 %all-gather.7.cloned.1.call-start = ((), (), s32[]{:S(2)}) async-start(), calls=%async_computation.2 | async-start | bytes 1179648 | tf_op jit(solution)/shard_map/all_gather | solution.py:119
  8.6 131.1 %all-gather.11.cloned.1.call-start = ((), (), s32[]{:S(2)}) async-start(), calls=%async_computation.4 | async-start | bytes 1179648 | tf_op jit(solution)/shard_map/all_gather | solution.py:137
  9.4 171.3 %all-gather.9.cloned.1.call-start = ((), (), s32[]{:S(2)}) async-start(), calls=%async_computation.3 | async-start | bytes 1179648 | tf_op jit(solution)/shard_map/all_gather | solution.py:136
  13.8 26.0 %all-to-all-start = ((bf16[8,32,1024]{2,1,0:T(8,128)(2,1)}), bf16[8,32,1024]{2,1,0:T(8,128)(2,1)S(1)}, u32[]{:S(2)}, u32[]{:S(2)}) async-start(bf16[8,32,1024]{2,1,0:T(8,128)(2,1)} %bitcast.16), calls=%async_computation | async-start | bytes 1048576 | tf_op jit(solution)/shard_map/all_to_all | solution.py:162
  98.6 82.1 %copy-start.1 = (s32[1024]{0:T(1024)S(1)}, s32[1024]{0:T(1024)}, u32[]{:S(2)}) copy-start(s32[1024]{0:T(1024)} %param.24) | copy-start | bytes 12292
  109.9 5.9 %copy-start = (f32[4,512,128,8]{2,1,3,0:T(8,128)S(1)}, f32[4,512,128,8]{2,1,3,0:T(8,128)}, u32[]{:S(2)}) copy-start(f32[4,512,128,8]{2,1,3,0:T(8,128)} %get-tuple-element.498) | copy-start | bytes 25165828 | tf_op jit(solution)/shard_map/cond/branch_1_fun/while
  126.6 6.9 %copy-start = (f32[4,512,128,8]{2,1,3,0:T(8,128)S(1)}, f32[4,512,128,8]{2,1,3,0:T(8,128)}, u32[]{:S(2)}) copy-start(f32[4,512,128,8]{2,1,3,0:T(8,128)} %get-tuple-element.498) | copy-start | bytes 25165828 | tf_op jit(solution)/shard_map/cond/branch_1_fun/while
Sparse Core Ops, SparseCore 0:
  10.1 47.3 all-gather.4
  59.7 38.8 all-gather.6
  100.7 38.9 all-gather.10
  141.7 38.8 all-gather.8
where the time goes:
time: 221 us; the launch traced here: 220 us
  waiting for transfers between devices  111 us (50%)
  matrix products  33.8 us (15%)
  other arithmetic  29.3 us (13%)
  local copies, waits for them, and re-layouts  22.6 us (10%)
  between operations  15.1 us (7%)
  starting transfers between devices  7.43 us (3%)
    all_gather x1, waiting for transfers between devices, shards(): piece_values = lax.all_gather(prefix_values, 'blk', axis=0, tiled=True)  41.1 us
    all_gather x1, waiting for transfers between devices, shards(): piece_keys = lax.all_gather(new_keys, 'blk', axis=0, tiled=True)  40.9 us
    dot_general x4, matrix products, one_block(): jnp.einsum('kgtn,nkd->kgtd', weights.astype(jnp.bfloat16), value_part, pr...  19.9 us
    all_gather x1, waiting for transfers between devices, shards(): piece_keys = lax.all_gather(prefix_keys, 'blk', axis=0, tiled=True)  17 us
    reduce_sum x4, other arithmetic, one_block(): running_sum = running_sum * rescale + jnp.sum(weights, axis=-1)  13.6 us
    dot_general x4, matrix products, one_block(): jnp.einsum('tkgd,nkd->kgtn', query_groups, key_part, preferred_element_ty...  11.9 us
    all_to_all x1, waiting for transfers between devices, shards(): lax.all_to_all(outgoing, 'blk', split_axis=0, concat_axis=0, tiled=True)  9.37 us
    all_to_all x1, starting transfers between devices, shards(): lax.all_to_all(outgoing, 'blk', split_axis=0, concat_axis=0, tiled=True)  7.28 us
  transfers between devices with their start and end apart: 5, of which 5 were waited for; matrix products, arithmetic and copies ran while one was open for 24% of the time, Pallas kernels for 0%

commit v1 on v0

--- a/solution.py
+++ b/solution.py
@@ -1,13 +1,289 @@
+import functools
 import math
 
 import jax
 import jax.numpy as jnp
 from jax import lax
+from jax.experimental import pallas as pl
+from jax.experimental.pallas import tpu as pltpu
 from jax.sharding import PartitionSpec as P
 
 H = 64
 KVH = 8
 HD = 128
+PIECE = 64
+LARGE_NEGATIVE = -1e30
+
+VMEM = pltpu.VMEM
+SMEM = pltpu.SMEM
+ANY = pl.ANY
+
+
+def dot_nt(a, b):
+    return lax.dot_general(a, b, (((1,), (1,)), ((), ())), preferred_element_type=jnp.float32)
+
+
+def dot_nn(a, b):
+    return lax.dot_general(a, b, (((1,), (0,)), ((), ())), preferred_element_type=jnp.float32)
+
+
+def stage_kernel(offsets, parts, first, last, rows, heads, groups, requests, capacity, *refs):
+    refs = list(refs)
+    me_ref, place_ref, span_ref, plen_ref, dest_ref, query_ref = refs[:6]
+    refs = refs[6:]
+    blocks = []
+    for count in parts:
+        blocks.append(refs[:count])
+        refs = refs[count:]
+    if not first:
+        max_in, acc_in = refs[:2]
+        refs = refs[4:]
+    if last:
+        att_ref, dkey_ref, dval_ref = refs[:3]
+        refs = refs[3:]
+        max_ref, acc_ref = max_in, acc_in
+    else:
+        max_ref, acc_ref, dkey_ref, dval_ref = refs[:4]
+        refs = refs[4:]
+    picked_ref, sems = refs
+    me = me_ref[0]
+    pieces = rows // PIECE
+    unit = groups * PIECE
+    factor = math.log2(math.e) / math.sqrt(HD)
+
+    def bounds(token):
+        low = jnp.zeros_like(token)
+        pre_low = jnp.zeros_like(token)
+        pre_high = jnp.zeros_like(token) + plen_ref[0]
+        end = jnp.int32(0)
+        for r in range(requests - 1):
+            end = end + span_ref[r]
+            past = token >= end
+            low = low + jnp.where(past, span_ref[r], 0)
+            pre_low = pre_low + jnp.where(past, plen_ref[r], 0)
+            pre_high = pre_high + jnp.where(past, plen_ref[r + 1], 0)
+        return low, pre_low, pre_high
+
+    def part_of(block, which, start, size):
+        if len(block) == 1:
+            return block[0][which * rows:(which + 1) * rows, pl.ds(start, size)]
+        half, inner = divmod(which, 2)
+        return block[half][inner * rows:(inner + 1) * rows, pl.ds(start, size)]
+
+    copies = []
+    for n, (offset, block) in enumerate(zip(offsets, blocks)):
+        index = me ^ offset
+        for piece in range(pieces):
+            base = place_ref[me * rows + piece * PIECE]
+            low0, pre0, unused = bounds(base)
+            unused, unused2, pre1 = bounds(base + (PIECE - 1))
+            seen = (pre0 < (index + 1) * rows) & (pre1 > index * rows)
+            for other in range(pieces):
+                there = place_ref[index * rows + other * PIECE]
+                seen = seen | ((there <= base) & (there + (PIECE - 1) >= low0))
+
+            def work(piece=piece, base=base, block=block, index=index, n=n):
+                token = base + lax.broadcasted_iota(jnp.int32, (PIECE, 1), 0)
+                low, pre_low, pre_high = bounds(token)
+                column = lax.broadcasted_iota(jnp.int32, (PIECE, rows), 1)
+                position = column + index * rows
+                pre_seen = (position >= pre_low) & (position < pre_high)
+                key_token = jnp.zeros((PIECE, rows), jnp.int32)
+                for other in range(pieces):
+                    there = place_ref[index * rows + other * PIECE] - other * PIECE
+                    key_token = jnp.where(column >= other * PIECE, column + there, key_token)
+                new_seen = (key_token >= low) & (key_token <= token)
+                bias = jnp.concatenate(
+                    [
+                        jnp.where(pre_seen, 0.0, LARGE_NEGATIVE),
+                        jnp.where(new_seen, 0.0, LARGE_NEGATIVE),
+                    ],
+                    axis=1,
+                ).astype(jnp.float32)
+                step = 4
+                for k in range(heads):
+                    keys = jnp.concatenate(
+                        [part_of(block, 0, k * HD, HD), part_of(block, 2, k * HD, HD)], axis=0
+                    )
+                    values = jnp.concatenate(
+                        [part_of(block, 1, k * HD, HD), part_of(block, 3, k * HD, HD)], axis=0
+                    )
+                    values = jnp.concatenate([values, jnp.ones_like(values)], axis=1)
+                    for g in range(0, groups, step):
+                        query = jnp.concatenate(
+                            [
+                                query_ref[
+                                    piece * PIECE:(piece + 1) * PIECE,
+                                    (k * groups + g + j) * HD:(k * groups + g + j + 1) * HD,
+                                ]
+                                for j in range(step)
+                            ],
+                            axis=0,
+                        )
+                        scores = dot_nt(query, keys) * factor
+                        scores = scores.reshape(step, PIECE, 2 * rows) + bias[None]
+                        scores = scores.reshape(step * PIECE, 2 * rows)
+                        at = slice(g * PIECE, (g + step) * PIECE)
+                        here = jnp.max(scores, axis=1, keepdims=True)
+                        if first and n == 0:
+                            new_max = jnp.broadcast_to(here, (step * PIECE, HD))
+                        else:
+                            source_max, source_acc = (
+                                (max_in, acc_in) if n == 0 and not first else (max_ref, acc_ref)
+                            )
+                            old_max = source_max[k, piece, at, :]
+                            new_max = jnp.maximum(old_max, here)
+                        weights = jnp.exp2(scores - jnp.concatenate([new_max, new_max], axis=1))
+                        added = dot_nn(weights.astype(jnp.bfloat16), values)
+                        if not (first and n == 0):
+                            rescale = jnp.exp2(old_max - new_max)
+                            rescale = jnp.concatenate([rescale, rescale], axis=1)
+                            added = source_acc[k, piece, at, :] * rescale + added
+                        acc_ref[k, piece, at, :] = added
+                        max_ref[k, piece, at, :] = new_max
+
+            if first and n == 0:
+                work()
+            else:
+                pl.when(seen)(work)
+        mine = jnp.where(dest_ref[pl.ds(index, 1), :] == me, 1.0, 0.0)
+        lane = lax.broadcasted_iota(jnp.int32, (rows, rows), 0)
+        lane2 = lax.broadcasted_iota(jnp.int32, (rows, rows), 1)
+        earlier = jnp.where(lane < lane2, 1.0, 0.0).astype(jnp.bfloat16)
+        mine = jnp.broadcast_to(mine, (capacity, rows))
+        rank = dot_nn(mine.astype(jnp.bfloat16), earlier)
+        slot = lax.broadcasted_iota(jnp.int32, (capacity, rows), 0).astype(jnp.float32)
+        choose = jnp.where((rank == slot) & (mine > 0.5), 1.0, 0.0).astype(jnp.bfloat16)
+        for which, out_ref in ((2, dkey_ref), (3, dval_ref)):
+            picked_ref[n, which - 2] = dot_nn(choose, part_of(block, which, 0, heads * HD)).astype(
+                jnp.bfloat16
+            )
+            copy = pltpu.make_async_copy(
+                picked_ref.at[n, which - 2],
+                out_ref.at[pl.ds(pl.multiple_of(index * capacity, capacity), capacity)],
+                sems.at[n, which - 2],
+            )
+            copy.start()
+            copies.append(copy)
+    if last:
+        for piece in range(pieces):
+            for k in range(heads):
+                for g in range(groups):
+                    both = acc_ref[k, piece, g * PIECE:(g + 1) * PIECE, :]
+                    att_ref[
+                        piece * PIECE:(piece + 1) * PIECE,
+                        (k * groups + g) * HD:(k * groups + g + 1) * HD,
+                    ] = (both[:, :HD] / both[:, HD:]).astype(jnp.bfloat16)
+    for copy in copies:
+        copy.wait()
+
+
+def run_stage(common, offsets, blocks, carry, last, capacity):
+    query = common[-1]
+    rows, columns = query.shape
+    groups = H // KVH
+    heads = columns // (groups * HD)
+    requests = common[2].shape[0]
+    pieces = rows // PIECE
+    first = carry is None
+    parts = tuple(len(block) for block in blocks)
+    flat = [ref for block in blocks for ref in block]
+    operands = list(common) + flat + (list(carry) if carry is not None else [])
+    specs = [pl.BlockSpec(memory_space=SMEM)] * 4 + [pl.BlockSpec(memory_space=VMEM)] * (2 + len(flat))
+    unit = groups * PIECE
+    max_shape = jax.ShapeDtypeStruct((heads, pieces, unit, HD), jnp.float32)
+    acc_shape = jax.ShapeDtypeStruct((heads, pieces, unit, 2 * HD), jnp.float32)
+    decode_shape = jax.ShapeDtypeStruct((capacity * (common[1].shape[0] // rows), heads * HD), jnp.bfloat16)
+    alias = {}
+    at = len(common) + len(flat)
+    if not first:
+        specs += [pl.BlockSpec(memory_space=VMEM)] * 2 + [pl.BlockSpec(memory_space=ANY)] * 2
+    if last:
+        out_shape = (jax.ShapeDtypeStruct((rows, columns), jnp.bfloat16), decode_shape, decode_shape)
+        out_specs = (pl.BlockSpec(memory_space=VMEM),) + (pl.BlockSpec(memory_space=ANY),) * 2
+        alias = {at + 2: 1, at + 3: 2}
+    else:
+        out_shape = (max_shape, acc_shape, decode_shape, decode_shape)
+        out_specs = (pl.BlockSpec(memory_space=VMEM),) * 2 + (pl.BlockSpec(memory_space=ANY),) * 2
+        if not first:
+            alias = {at + j: j for j in range(4)}
+    body = functools.partial(
+        stage_kernel, offsets, parts, first, last, rows, heads, groups, requests, capacity
+    )
+    keys = 2 * rows * len(blocks)
+    return pl.pallas_call(
+        body,
+        out_shape=out_shape,
+        in_specs=specs,
+        out_specs=out_specs,
+        input_output_aliases=alias,
+        scratch_shapes=[
+            VMEM((len(blocks), 2, capacity, heads * HD), jnp.bfloat16),
+            pltpu.SemaphoreType.DMA((len(blocks), 2)),
+        ],
+        compiler_params=pltpu.CompilerParams(vmem_limit_bytes=20 * 1024 * 1024),
+        cost_estimate=pl.CostEstimate(
+            flops=4 * rows * columns * keys, bytes_accessed=4 * 1024 * 1024, transcendentals=0
+        ),
+    )(*operands)
+
+
+def together(values, *after):
+    return lax.optimization_barrier(tuple(values) + after)[: len(values)]
+
+
+def cycle_of_eight(
+    queries, new_keys, new_values, prefix_keys, prefix_values, span_lens, prefix_lens, placement, decode_dest
+):
+    cycle = lax.axis_size("blk")
+    me = lax.axis_index("blk")
+    rows = queries.shape[0]
+    capacity = 2 * rows // cycle
+    place = me // 2
+    outer = (place == 0) | (place == 3)
+
+    def moves(table):
+        return [(2 * a + y, 2 * b + y) for a, b in table.items() for y in range(2)]
+
+    swap = [(i, i ^ 1) for i in range(cycle)]
+    near = moves({0: 1, 1: 0, 2: 3, 3: 2})
+    middle = moves({1: 2, 2: 1})
+    ends = moves({0: 3, 3: 0})
+    skip = moves({0: 2, 3: 1, 2: 3, 1: 0})
+    send = lambda x, table: lax.ppermute(x, "blk", table)
+
+    common = (
+        me.astype(jnp.int32)[None],
+        placement,
+        span_lens,
+        prefix_lens,
+        decode_dest.reshape(cycle, rows),
+        queries,
+    )
+    own = jnp.concatenate([prefix_keys, prefix_values, new_keys, new_values], axis=0)
+    half = own.shape[0] // 2
+
+    a = send(own, near)
+    y_own = send(own, swap)
+    b_inner = send(own, middle)
+    carry = run_stage(common, (0,), [[own]], None, False, capacity)
+
+    own_2, a_2, y_own_2, *carry = together((own, a, y_own) + tuple(carry))
+    b_outer = send(own_2, ends)
+    y_a = send(a_2, swap)
+    carry = run_stage(common, (2, 1), [[a_2], [y_own_2]], carry, False, capacity)
+
+    b = jnp.where(outer, b_outer, b_inner)
+    skip_from, b, y_a, *carry = together((jnp.where(outer, own_2, b_inner), b, y_a) + tuple(carry))
+    c = send(skip_from, skip)
+    y_b = send(b, swap)
+    carry = run_stage(common, (6, 3), [[b], [y_a]], carry, False, capacity)
+
+    c, y_b, *carry = together((c, y_b) + tuple(carry))
+    y_c_low = send(c[:half], swap)
+    y_c_high = send(y_b[half:], near)
+    carry = run_stage(common, (4, 7), [[c], [y_b]], carry, False, capacity)
+    return run_stage(common, (5,), [[y_c_low, y_c_high]], carry, True, capacity)
 
 
 masked_score = -1e30
@@ -84,7 +360,7 @@
     )
 
 
-def shards(
+def any_cycle(
     queries,
     new_keys,
     new_values,
@@ -171,25 +447,11 @@
 
 
 def solution(mesh):
-    placed = (
-        P(("groups", "blk"), "tensor"),
-        P(("groups", "blk"), "tensor"),
-        P(("groups", "blk"), "tensor"),
-        P(("groups", "blk"), "tensor"),
-        P(("groups", "blk"), "tensor"),
-        P("groups"),
-        P("groups"),
-        P("groups"),
-        P("groups", None),
-    )
+    rows = P(("groups", "blk"), "tensor")
     return jax.shard_map(
-        shards,
+        cycle_of_eight if mesh.shape["blk"] == 8 else any_cycle,
         mesh=mesh,
-        in_specs=placed,
-        out_specs=(
-            P(("groups", "blk"), "tensor"),
-            P(("groups", "blk"), "tensor"),
-            P(("groups", "blk"), "tensor"),
-        ),
+        in_specs=(rows,) * 5 + (P("groups"),) * 3 + (P("groups", None),),
+        out_specs=(rows,) * 3,
         check_vma=False,
     )

time: 221 us -> 67.4 us (0.30)
  waiting for transfers between devices: 111 us -> 5.88 us
  matrix products: 33.8 us -> 0 us
  Pallas kernels: 0 us -> 29.3 us
  other arithmetic: 29.3 us -> 1.3 us
  between operations: 15.1 us -> 0.93 us
  starting transfers between devices: 7.43 us -> 15.2 us
  local copies, waits for them, and re-layouts: 22.6 us -> 15.6 us
    all_gather x4 -> x0, waiting for transfers between devices: 99.3 us -> none  [the longest x1 41.1 us: shards(): piece_values = lax.all_gather(prefix_values, 'blk', axis=0, tiled=True)]
    dot_general x9 -> x0, matrix products: 33.8 us -> none  [the longest x4 19.9 us: one_block(): jnp.einsum('kgtn,nkd->kgtd', weights.astype(jnp.bfloat16), value_part, pr...]
    pallas_call x0 -> x5, Pallas kernels: none -> 29.3 us  [run_stage(): pl.pallas_call(body, out_shape=out_shape, in_specs=specs, out_specs=out_s...]
    ppermute x0 -> x9, starting transfers between devices: none -> 15.2 us  [cycle_of_eight(): send = lambda x, table: lax.ppermute(x, 'blk', table)]
    reduce_sum x8 -> x0, other arithmetic: 14.7 us -> none  [the longest x4 13.6 us: one_block(): running_sum = running_sum * rescale + jnp.sum(weights, axis=-1)]
    unnamed x4 -> x27, local copies, waits for them, and re-layouts: 3.68 us -> 14.7 us
    all_to_all x1 -> x0, waiting for transfers between devices: 9.37 us -> none  [shards(): lax.all_to_all(outgoing, 'blk', split_axis=0, concat_axis=0, tiled=True)]
    all_to_all x1 -> x0, starting transfers between devices: 7.28 us -> none  [shards(): lax.all_to_all(outgoing, 'blk', split_axis=0, concat_axis=0, tiled=True)]
  transfers between devices with their start and end apart: 5 -> 9, of which waited for: 5 -> 4; matrix products, arithmetic and copies ran while one was open for 24% -> 2% of each run, Pallas kernels for 0% -> 36%
where the time goes in v1:
time: 67.4 us; the launch traced here: 68.2 us
  Pallas kernels  29.3 us (43%)
  local copies, waits for them, and re-layouts  15.6 us (23%)
  starting transfers between devices  15.2 us (23%)
  waiting for transfers between devices  5.88 us (9%)
  other arithmetic  1.3 us (2%)
  between operations  0.93 us (1%)
    pallas_call x5, Pallas kernels, run_stage(): pl.pallas_call(body, out_shape=out_shape, in_specs=specs, out_specs=out_s...  29.3 us
    ppermute x9, starting transfers between devices, cycle_of_eight(): send = lambda x, table: lax.ppermute(x, 'blk', table)  15.2 us
    unnamed x27, local copies, waits for them, and re-layouts  14.7 us
    ppermute x9, waiting for transfers between devices, cycle_of_eight(): send = lambda x, table: lax.ppermute(x, 'blk', table)  5.88 us
  transfers between devices with their start and end apart: 9, of which 4 were waited for; matrix products, arithmetic and copies ran while one was open for 2% of the time, Pallas kernels for 36%

profile of v1, /device:TPU:0, one launch (start us, length us, event | category | flops | bytes accessed | tf_op | source)
XLA Modules:
  0.0 68.2 jit_solution(11046640334297051115)
XLA Ops:
  0.6 0.9 %constant_dynamic-update-slice_fusion.3 = bf16[512,512]{1,0:T(8,128)(2,1)S(1)} fusion(bf16[128,512]{1,0:T(8,128)(2,1)} %param.12), kind=kLoop, calls=%fused_computation.5 | loop fusion | bytes 262144
  1.5 0.9 %constant_dynamic-update-slice_fusion.2 = bf16[512,512]{1,0:T(8,128)(2,1)S(1)} fusion(bf16[512,512]{1,0:T(8,128)(2,1)S(1)} %constant_dynamic-update-slice_fusion.3, bf16[128,512]{1,0:T(8,128)(2,1)} %param.13), kind=kLoop, calls=%fused_computation.4 | loop fusion | bytes 262144
  2.5 0.9 %constant_dynamic-update-slice_fusion.1 = bf16[512,512]{1,0:T(8,128)(2,1)S(1)} fusion(bf16[512,512]{1,0:T(8,128)(2,1)S(1)} %constant_dynamic-update-slice_fusion.2, bf16[128,512]{1,0:T(8,128)(2,1)} %param.10), kind=kLoop, calls=%fused_computation.3 | loop fusion | bytes 262144
  3.4 0.9 %constant_dynamic-update-slice_fusion.refs_6_ = bf16[512,512]{1,0:T(8,128)(2,1)S(1)} fusion(bf16[512,512]{1,0:T(8,128)(2,1)S(1)} %constant_dynamic-update-slice_fusion.1, bf16[128,512]{1,0:T(8,128)(2,1)} %param.11), kind=kLoop, calls=%fused_computation.2 | loop fusion | bytes 262144 | tf_op jit(solution)/shard_map/concatenate | solution.py:263
  4.3 3.1 %collective-permute-start = (bf16[512,512]{1,0:T(8,128)(2,1)S(1)}, bf16[512,512]{1,0:T(8,128)(2,1)S(1)}, u32[]{:S(2)}, u32[]{:S(2)}) collective-permute-start(bf16[512,512]{1,0:T(8,128)(2,1)S(1)} %constant_dynamic-update-slice_fusion.refs_6_), channel_id=1, source_target_pairs={{0,4},{2,6},{4,0},{6,2},{8,12},{10,14},{12,8},{14,10},{1,5},{3,7},... | collective-permute-start | bytes 1572872 | tf_op jit(solution)/shard_map/ppermute | solution.py:253
  7.4 1.5 %collective-permute-start.1 = (bf16[512,512]{1,0:T(8,128)(2,1)S(1)}, bf16[512,512]{1,0:T(8,128)(2,1)}, u32[]{:S(2)}, u32[]{:S(2)}) collective-permute-start(bf16[512,512]{1,0:T(8,128)(2,1)S(1)} %constant_dynamic-update-slice_fusion.refs_6_), channel_id=1, source_target_pairs={{0,2},{2,0},{4,6},{6,4},{8,10},{10,8},{12,14},{14,12},{1,3},{3,1},... | collective-permute-start | bytes 1572872 | tf_op jit(solution)/shard_map/ppermute | solution.py:253
  8.9 1.5 %collective-permute-start.2 = (bf16[512,512]{1,0:T(8,128)(2,1)S(1)}, bf16[512,512]{1,0:T(8,128)(2,1)}, u32[]{:S(2)}, u32[]{:S(2)}) collective-permute-start(bf16[512,512]{1,0:T(8,128)(2,1)S(1)} %constant_dynamic-update-slice_fusion.refs_6_), channel_id=1, source_target_pairs={{4,8},{6,10},{8,4},{10,6},{5,9},{7,11},{9,5},{11,7},{20,24},{22,26... | collective-permute-start | bytes 1572872 | tf_op jit(solution)/shard_map/ppermute | solution.py:253
  10.4 0.0 copy-start.2
  10.4 1.2 %copy-done.2 = bf16[128,4096]{1,0:T(8,128)(2,1)S(1)} copy-done((bf16[128,4096]{1,0:T(8,128)(2,1)S(1)}, bf16[128,4096]{1,0:T(8,128)(2,1)}, u32[]{:S(2)}) %copy-start.2) | copy-done | bytes 1048600
  11.6 0.0 copy-start.4
  11.6 0.7 %copy-done.4 = s32[1024]{0:T(1024)S(1)} copy-done((s32[1024]{0:T(1024)S(1)}, s32[1024]{0:T(1024)}, u32[]{:S(2)}) %copy-start.4) | copy-done | bytes 4120
  12.3 0.0 copy-start.6
  12.3 0.7 %copy-done.6 = s32[1024,1]{0,1:T(1,128)S(1)} copy-done((s32[1024,1]{0,1:T(1,128)S(1)}, s32[1024,1]{0,1:T(1,128)}, u32[]{:S(2)}) %copy-start.6) | copy-done | bytes 4120
  13.0 0.0 copy-start.8
  13.0 0.7 copy-done.8
  13.6 0.0 copy-start.10
  13.6 0.7 copy-done.10
  14.3 2.8 %shard_map.112 = (f32[4,2,512,128]{3,2,1,0:T(8,128)S(1)}, f32[4,2,512,256]{3,2,1,0:T(8,128)S(1)}, bf16[256,512]{1,0:T(8,128)(2,1)}, bf16[256,512]{1,0:T(8,128)(2,1)}) custom-call(s32[1]{0:T(128)} %bitcast.refs_0_, s32[1024]{0:T(1024)S(1)} %copy-done.4, s32[2]{0:T(128)S(1)} %copy-done.8, s32[2]{0:T(128)S(1)} %copy-done.10, s32[8,128]{1,0:T(8,128)S(1)} %bitcast.2, ...), custom_call_target="tpu_custom_call" | custom-call | flops 536870912 | bytes 4194304 | tf_op jit(solution)/shard_map/pallas_call | solution.py:214
  17.0 0.0 copy-start
  17.1 1.9 %copy-done = f32[4,2,512,256]{3,2,1,0:T(8,128)} copy-done((f32[4,2,512,256]{3,2,1,0:T(8,128)}, f32[4,2,512,256]{3,2,1,0:T(8,128)S(1)}, u32[]{:S(2)}) %copy-start) | copy-done | bytes 4194328
  19.0 0.3 collective-permute-done.refs_6_
  19.3 1.6 %collective-permute-done.1.refs_7_ = bf16[512,512]{1,0:T(8,128)(2,1)} collective-permute-done((bf16[512,512]{1,0:T(8,128)(2,1)S(1)}, bf16[512,512]{1,0:T(8,128)(2,1)}, u32[]{:S(2)}, u32[]{:S(2)}) %collective-permute-start.1) | collective-permute-done | bytes 524320 | tf_op jit(solution)/shard_map/ppermute | solution.py:253
  20.9 4.4 %collective-permute-start.3 = (bf16[512,512]{1,0:T(8,128)(2,1)S(1)}, bf16[512,512]{1,0:T(8,128)(2,1)}, u32[]{:S(2)}, u32[]{:S(2)}) collective-permute-start(bf16[512,512]{1,0:T(8,128)(2,1)S(1)} %constant_dynamic-update-slice_fusion.refs_6_), channel_id=1, source_target_pairs={{0,12},{2,14},{12,0},{14,2},{1,13},{3,15},{13,1},{15,3},{16,28},{1... | collective-permute-start | bytes 1572872 | tf_op jit(solution)/shard_map/ppermute | solution.py:253
  25.3 1.6 %collective-permute-start.4 = (bf16[512,512]{1,0:T(8,128)(2,1)S(1)}, bf16[512,512]{1,0:T(8,128)(2,1)}, u32[]{:S(2)}, u32[]{:S(2)}) collective-permute-start(bf16[512,512]{1,0:T(8,128)(2,1)S(1)} %collective-permute-done.refs_6_), channel_id=1, source_target_pairs={{0,2},{2,0},{4,6},{6,4},{8,10},{10,8},{12,14},{14,12},{1,3},{3,1},... | collective-permute-start | bytes 1572872 | tf_op jit(solution)/shard_map/ppermute | solution.py:253
  26.8 0.0 copy-start.1
  26.9 2.2 %copy-done.1 = f32[4,2,512,256]{3,2,1,0:T(8,128)S(1)} copy-done((f32[4,2,512,256]{3,2,1,0:T(8,128)S(1)}, f32[4,2,512,256]{3,2,1,0:T(8,128)}, u32[]{:S(2)}) %copy-start.1) | copy-done | bytes 4194328
  29.0 0.0 copy-start.3
  29.0 1.2 %copy-done.3 = bf16[128,4096]{1,0:T(8,128)(2,1)S(1)} copy-done((bf16[128,4096]{1,0:T(8,128)(2,1)S(1)}, bf16[128,4096]{1,0:T(8,128)(2,1)}, u32[]{:S(2)}) %copy-start.3) | copy-done | bytes 1048600
  30.3 0.7 %copy-done.5 = s32[1024]{0:T(1024)S(1)} copy-done((s32[1024]{0:T(1024)S(1)}, s32[1024]{0:T(1024)}, u32[]{:S(2)}) %copy-start.5) | copy-done | bytes 4120
  31.0 0.7 %copy-done.7 = s32[1024,1]{0,1:T(1,128)S(1)} copy-done((s32[1024,1]{0,1:T(1,128)S(1)}, s32[1024,1]{0,1:T(1,128)}, u32[]{:S(2)}) %copy-start.7) | copy-done | bytes 4120
  31.6 0.7 copy-done.9
  32.3 0.7 copy-done.11
  32.9 7.4 %shard_map.113 = (f32[4,2,512,128]{3,2,1,0:T(8,128)S(1)}, f32[4,2,512,256]{3,2,1,0:T(8,128)S(1)}, bf16[256,512]{1,0:T(8,128)(2,1)}, bf16[256,512]{1,0:T(8,128)(2,1)}) custom-call(s32[1]{0:T(128)} %bitcast.refs_0_, s32[1024]{0:T(1024)S(1)} %copy-done.5, s32[2]{0:T(128)S(1)} %copy-done.9, ...), custom_call_target="tpu_custom_call", output_to_operand_aliasing={{0}: (8, {}), {1}: (9, {}), {2}: (10, {}), {3}: (11, {})} | custom-call | flops 1073741824 | bytes 4194304 | tf_op jit(solution)/shard_map/pallas_call | solution.py:214
  40.4 0.0 collective-permute-done.2
  40.4 0.0 collective-permute-done.3
  40.4 1.3 %broadcast_select_fusion = (bf16[512,512]{1,0:T(8,128)(2,1)S(1)}, bf16[512,512]{1,0:T(8,128)(2,1)S(1)}) fusion(bf16[512,512]{1,0:T(8,128)(2,1)} %collective-permute-done.3, bf16[512,512]{1,0:T(8,128)(2,1)} %collective-permute-done.2, pred[]{:T(512)S(6)} %or.3, bf16[512,512]{1,0:T(8,128)(2,1)S(1)} %constant_dynamic-update-slice_fusion.refs_6_), kind=kLoop, calls=%fused_computation | loop fusion | flops 524288 | bytes 2621441 | tf_op jit(solution)/shard_map/jit(_where)/select_n | solution.py:276
  41.7 0.0 collective-permute-done.4.refs_7_
  41.7 0.1 collective-permute-start.5
  41.8 0.6 collective-permute-start.6
  42.3 7.6 %shard_map.114 = (f32[4,2,512,128]{3,2,1,0:T(8,128)S(1)}, f32[4,2,512,256]{3,2,1,0:T(8,128)S(1)}, bf16[256,512]{1,0:T(8,128)(2,1)}, bf16[256,512]{1,0:T(8,128)(2,1)}) custom-call(s32[1]{0:T(128)} %bitcast.refs_0_, s32[1024]{0:T(1024)S(1)} %copy-done.5, s32[2]{0:T(128)S(1)} %copy-done.9, ...), custom_call_target="tpu_custom_call", output_to_operand_aliasing={{0}: (8, {}), {1}: (9, {}), {2}: (10, {}), {3}: (11, {})} | custom-call | flops 1073741824 | bytes 4194304 | tf_op jit(solution)/shard_map/pallas_call | solution.py:214
  49.9 3.9 %collective-permute-done.5.refs_6_ = bf16[512,512]{1,0:T(8,128)(2,1)S(1)} collective-permute-done((bf16[512,512]{1,0:T(8,128)(2,1)S(1)}, bf16[512,512]{1,0:T(8,128)(2,1)S(1)}, u32[]{:S(2)}, u32[]{:S(2)}) %collective-permute-start.5) | collective-permute-done | bytes 524320 | tf_op jit(solution)/shard_map/ppermute | solution.py:253
  53.8 0.1 collective-permute-done.6.refs_7_
  53.9 0.6 collective-permute-start.7
  54.5 2.0 %collective-permute-start.8 = (bf16[256,512]{1,0:T(8,128)(2,1)S(1)}, bf16[256,512]{1,0:T(8,128)(2,1)S(1)}, u32[]{:S(2)}, u32[]{:S(2)}) collective-permute-start(bf16[256,512]{1,0:T(8,128)(2,1)S(1)} %slice.7), channel_id=1, source_target_pairs={{0,4},{2,6},{4,0},{6,2},{8,12},{10,14},{12,8},{14,10},{1,5},{3,7},... | collective-permute-start | bytes 786440 | tf_op jit(solution)/shard_map/ppermute | solution.py:253
  56.5 7.0 %shard_map.115 = (f32[4,2,512,128]{3,2,1,0:T(8,128)S(1)}, f32[4,2,512,256]{3,2,1,0:T(8,128)S(1)}, bf16[256,512]{1,0:T(8,128)(2,1)}, bf16[256,512]{1,0:T(8,128)(2,1)}) custom-call(s32[1]{0:T(128)} %bitcast.refs_0_, s32[1024]{0:T(1024)S(1)} %copy-done.5, s32[2]{0:T(128)S(1)} %copy-done.9, ...), custom_call_target="tpu_custom_call", output_to_operand_aliasing={{0}: (8, {}), {1}: (9, {}), {2}: (10, {}), {3}: (11, {})} | custom-call | flops 1073741824 | bytes 4194304 | tf_op jit(solution)/shard_map/pallas_call | solution.py:214
  63.4 0.0 collective-permute-done.7.refs_6_
  63.4 0.0 collective-permute-done.8.refs_7_
  63.4 4.6 %shard_map.116 = (bf16[128,4096]{1,0:T(8,128)(2,1)}, bf16[256,512]{1,0:T(8,128)(2,1)}, bf16[256,512]{1,0:T(8,128)(2,1)}) custom-call(s32[1]{0:T(128)} %bitcast.refs_0_, s32[1024]{0:T(1024)S(1)} %copy-done.5, s32[2]{0:T(128)S(1)} %copy-done.9, s32[2]{0:T(128)S(1)} %copy-done.11, ...), custom_call_target="tpu_custom_call", output_to_operand_aliasing={{1}: (10, {}), {2}: (11, {})} | custom-call | flops 536870912 | bytes 4194304 | tf_op jit(solution)/shard_map/pallas_call | solution.py:214
  (6 shorter events, 0.0 us)
Async XLA Ops:
  4.3 15.0 %collective-permute-start = (bf16[512,512]{1,0:T(8,128)(2,1)S(1)}, bf16[512,512]{1,0:T(8,128)(2,1)S(1)}, u32[]{:S(2)}, u32[]{:S(2)}) collective-permute-start(bf16[512,512]{1,0:T(8,128)(2,1)S(1)} %constant_dynamic-update-slice_fusion.refs_6_), channel_id=1, source_target_pairs={{0,4},{2,6},{4,0},{6,2},{8,12},{10,14},{12,8},{14,10},{1,5},{3,7},... | collective-permute-start | bytes 1572872 | tf_op jit(solution)/shard_map/ppermute | solution.py:253
  7.4 13.5 %collective-permute-start.1 = (bf16[512,512]{1,0:T(8,128)(2,1)S(1)}, bf16[512,512]{1,0:T(8,128)(2,1)}, u32[]{:S(2)}, u32[]{:S(2)}) collective-permute-start(bf16[512,512]{1,0:T(8,128)(2,1)S(1)} %constant_dynamic-update-slice_fusion.refs_6_), channel_id=1, source_target_pairs={{0,2},{2,0},{4,6},{6,4},{8,10},{10,8},{12,14},{14,12},{1,3},{3,1},... | collective-permute-start | bytes 1572872 | tf_op jit(solution)/shard_map/ppermute | solution.py:253
  8.9 31.4 %collective-permute-start.2 = (bf16[512,512]{1,0:T(8,128)(2,1)S(1)}, bf16[512,512]{1,0:T(8,128)(2,1)}, u32[]{:S(2)}, u32[]{:S(2)}) collective-permute-start(bf16[512,512]{1,0:T(8,128)(2,1)S(1)} %constant_dynamic-update-slice_fusion.refs_6_), channel_id=1, source_target_pairs={{4,8},{6,10},{8,4},{10,6},{5,9},{7,11},{9,5},{11,7},{20,24},{22,26... | collective-permute-start | bytes 1572872 | tf_op jit(solution)/shard_map/ppermute | solution.py:253
  10.4 1.2 %copy-start.2 = (bf16[128,4096]{1,0:T(8,128)(2,1)S(1)}, bf16[128,4096]{1,0:T(8,128)(2,1)}, u32[]{:S(2)}) copy-start(bf16[128,4096]{1,0:T(8,128)(2,1)} %refs_5_.9) | copy-start | bytes 3145732
  11.6 0.7 %copy-start.4 = (s32[1024]{0:T(1024)S(1)}, s32[1024]{0:T(1024)}, u32[]{:S(2)}) copy-start(s32[1024]{0:T(1024)} %refs_1_.9) | copy-start | bytes 12292
  12.3 0.7 %copy-start.6 = (s32[1024,1]{0,1:T(1,128)S(1)}, s32[1024,1]{0,1:T(1,128)}, u32[]{:S(2)}) copy-start(s32[1024,1]{0,1:T(1,128)} %param.17) | copy-start | bytes 12292
  13.0 0.7 copy-start.8
  13.6 0.7 copy-start.10
  17.0 1.9 %copy-start = (f32[4,2,512,256]{3,2,1,0:T(8,128)}, f32[4,2,512,256]{3,2,1,0:T(8,128)S(1)}, u32[]{:S(2)}) copy-start(f32[4,2,512,256]{3,2,1,0:T(8,128)S(1)} %get-tuple-element.47.refs_9_) | copy-start | bytes 12582916
  20.9 19.5 %collective-permute-start.3 = (bf16[512,512]{1,0:T(8,128)(2,1)S(1)}, bf16[512,512]{1,0:T(8,128)(2,1)}, u32[]{:S(2)}, u32[]{:S(2)}) collective-permute-start(bf16[512,512]{1,0:T(8,128)(2,1)S(1)} %constant_dynamic-update-slice_fusion.refs_6_), channel_id=1, source_target_pairs={{0,12},{2,14},{12,0},{14,2},{1,13},{3,15},{13,1},{15,3},{16,28},{1... | collective-permute-start | bytes 1572872 | tf_op jit(solution)/shard_map/ppermute | solution.py:253
  25.3 16.4 %collective-permute-start.4 = (bf16[512,512]{1,0:T(8,128)(2,1)S(1)}, bf16[512,512]{1,0:T(8,128)(2,1)}, u32[]{:S(2)}, u32[]{:S(2)}) collective-permute-start(bf16[512,512]{1,0:T(8,128)(2,1)S(1)} %collective-permute-done.refs_6_), channel_id=1, source_target_pairs={{0,2},{2,0},{4,6},{6,4},{8,10},{10,8},{12,14},{14,12},{1,3},{3,1},... | collective-permute-start | bytes 1572872 | tf_op jit(solution)/shard_map/ppermute | solution.py:253
  26.8 2.2 %copy-start.1 = (f32[4,2,512,256]{3,2,1,0:T(8,128)S(1)}, f32[4,2,512,256]{3,2,1,0:T(8,128)}, u32[]{:S(2)}) copy-start(f32[4,2,512,256]{3,2,1,0:T(8,128)} %copy-done) | copy-start | bytes 12582916
  29.0 1.2 %copy-start.3 = (bf16[128,4096]{1,0:T(8,128)(2,1)S(1)}, bf16[128,4096]{1,0:T(8,128)(2,1)}, u32[]{:S(2)}) copy-start(bf16[128,4096]{1,0:T(8,128)(2,1)} %refs_5_.9) | copy-start | bytes 3145732
  30.3 0.7 %copy-start.5 = (s32[1024]{0:T(1024)S(1)}, s32[1024]{0:T(1024)}, u32[]{:S(2)}) copy-start(s32[1024]{0:T(1024)} %refs_1_.9) | copy-start | bytes 12292
  30.9 0.7 %copy-start.7 = (s32[1024,1]{0,1:T(1,128)S(1)}, s32[1024,1]{0,1:T(1,128)}, u32[]{:S(2)}) copy-start(s32[1024,1]{0,1:T(1,128)} %param.17) | copy-start | bytes 12292
  31.6 0.7 copy-start.9
  32.3 0.7 copy-start.11
  41.7 12.1 %collective-permute-start.5 = (bf16[512,512]{1,0:T(8,128)(2,1)S(1)}, bf16[512,512]{1,0:T(8,128)(2,1)S(1)}, u32[]{:S(2)}, u32[]{:S(2)}) collective-permute-start(bf16[512,512]{1,0:T(8,128)(2,1)S(1)} %get-tuple-element.54), channel_id=1, source_target_pairs={{0,8},{2,10},{12,4},{14,6},{8,12},{10,14},{4,0},{6,2},{1,9},{3,11}... | collective-permute-start | bytes 1572872 | tf_op jit(solution)/shard_map/ppermute | solution.py:253
  41.8 12.1 %collective-permute-start.6 = (bf16[512,512]{1,0:T(8,128)(2,1)S(1)}, bf16[512,512]{1,0:T(8,128)(2,1)S(1)}, u32[]{:S(2)}, u32[]{:S(2)}) collective-permute-start(bf16[512,512]{1,0:T(8,128)(2,1)S(1)} %get-tuple-element.55.refs_6_), channel_id=1, source_target_pairs={{0,2},{2,0},{4,6},{6,4},{8,10},{10,8},{12,14},{14,12},{1,3},{3,1},... | collective-permute-start | bytes 1572872 | tf_op jit(solution)/shard_map/ppermute | solution.py:253
  53.9 9.5 %collective-permute-start.7 = (bf16[256,512]{1,0:T(8,128)(2,1)S(1)}, bf16[256,512]{1,0:T(8,128)(2,1)S(1)}, u32[]{:S(2)}, u32[]{:S(2)}) collective-permute-start(bf16[256,512]{1,0:T(8,128)(2,1)S(1)} %slice.6), channel_id=1, source_target_pairs={{0,2},{2,0},{4,6},{6,4},{8,10},{10,8},{12,14},{14,12},{1,3},{3,1},... | collective-permute-start | bytes 786440 | tf_op jit(solution)/shard_map/ppermute | solution.py:253
  54.5 8.9 %collective-permute-start.8 = (bf16[256,512]{1,0:T(8,128)(2,1)S(1)}, bf16[256,512]{1,0:T(8,128)(2,1)S(1)}, u32[]{:S(2)}, u32[]{:S(2)}) collective-permute-start(bf16[256,512]{1,0:T(8,128)(2,1)S(1)} %slice.7), channel_id=1, source_target_pairs={{0,4},{2,6},{4,0},{6,2},{8,12},{10,14},{12,8},{14,10},{1,5},{3,7},... | collective-permute-start | bytes 786440 | tf_op jit(solution)/shard_map/ppermute | solution.py:253

commit v2 on v0

--- a/solution.py
+++ b/solution.py
@@ -1,13 +1,435 @@
+import functools
 import math
 
 import jax
 import jax.numpy as jnp
 from jax import lax
+from jax.experimental import pallas as pl
+from jax.experimental.pallas import tpu as pltpu
 from jax.sharding import PartitionSpec as P
 
 H = 64
 KVH = 8
 HD = 128
+PIECE = 64
+LARGE_NEGATIVE = -1e30
+
+VMEM = pltpu.VMEM
+SMEM = pltpu.SMEM
+HBM = pltpu.HBM
+
+
+def dot_nt(a, b):
+    return lax.dot_general(a, b, (((1,), (1,)), ((), ())), preferred_element_type=jnp.float32)
+
+
+def dot_nn(a, b):
+    return lax.dot_general(a, b, (((1,), (0,)), ((), ())), preferred_element_type=jnp.float32)
+
+
+def part_of(block, which, rows, start, size):
+    if len(block) == 1:
+        return block[0][which * rows:(which + 1) * rows, start:start + size]
+    half, inner = divmod(which, 2)
+    return block[half][inner * rows:(inner + 1) * rows, start:start + size]
+
+
+def add_blocks(blocks, biases, query_ref, before, after, heads, groups, store):
+    rows = query_ref.shape[0]
+    factor = math.log2(math.e) / math.sqrt(HD)
+    step = 2
+    for k in range(heads):
+        keys, values = [], []
+        for block in blocks:
+            keys.append(
+                jnp.concatenate(
+                    [part_of(block, j, rows, k * HD, HD) for j in (0, 2)], axis=0
+                )
+            )
+            value = jnp.concatenate(
+                [part_of(block, j, rows, k * HD, HD) for j in (1, 3)], axis=0
+            )
+            values.append(jnp.concatenate([value, jnp.ones_like(value)], axis=1))
+        for g in range(0, groups, step):
+            query = jnp.concatenate(
+                [
+                    query_ref[:, (k * groups + g + j) * HD:(k * groups + g + j + 1) * HD]
+                    for j in range(step)
+                ],
+                axis=0,
+            )
+            at = slice(g * rows, (g + step) * rows)
+            scores = []
+            for key, bias in zip(keys, biases):
+                score = (dot_nt(query, key) * factor).reshape(step, rows, 2 * rows) + bias[...][None]
+                scores.append(score.reshape(step * rows, 2 * rows))
+            largest = functools.reduce(jnp.maximum, scores)
+            new_max = jnp.broadcast_to(
+                jnp.max(largest, axis=1, keepdims=True), (step * rows, HD)
+            )
+            if before is not None:
+                old_max = before[0][k, at, :]
+                new_max = jnp.maximum(old_max, new_max)
+            both_max = jnp.concatenate([new_max, new_max], axis=1)
+            added = None
+            for score, value in zip(scores, values):
+                weights = jnp.exp2(score - both_max).astype(jnp.bfloat16)
+                term = dot_nn(weights, value)
+                added = term if added is None else added + term
+            if before is not None:
+                rescale = jnp.exp2(old_max - new_max)
+                rescale = jnp.concatenate([rescale, rescale], axis=1)
+                added = before[1][k, at, :] * rescale + added
+            if after is not None:
+                after[0][k, at, :] = new_max
+                after[1][k, at, :] = added
+            else:
+                for j in range(step):
+                    both = added[j * rows:(j + 1) * rows]
+                    store(k, g + j, both[:, :HD] / both[:, HD:])
+        if after is None:
+            store(k, None, None)
+
+
+def pick_rows(offsets, blocks, choose_refs, out_refs, picked_ref, sems):
+    me = lax.axis_index("blk")
+    copies = []
+    for n, (offset, block, choose_ref) in enumerate(zip(offsets, blocks, choose_refs)):
+        capacity, rows = choose_ref.shape
+        index = me ^ offset
+        for which, out_ref in enumerate(out_refs):
+            new = part_of(block, 2 + which, rows, 0, out_ref.shape[1])
+            picked_ref[n, which] = dot_nn(choose_ref[...], new).astype(jnp.bfloat16)
+            copy = pltpu.make_async_copy(
+                picked_ref.at[n, which],
+                out_ref.at[pl.ds(pl.multiple_of(index * capacity, capacity), capacity)],
+                sems.at[n, which],
+            )
+            copy.start()
+            copies.append(copy)
+    return copies
+
+
+def first_kernel(
+    offsets, rows, heads, groups, requests, capacity,
+    place_in, span_in, plen_in, dest_in, query_in, own_ref,
+    max_ref, acc_ref, dkey_ref, dval_ref, query_ref, bias_ref, choose_ref,
+    place_ref, span_ref, plen_ref, dest_ref, picked_ref, sems, small_sems,
+):
+    small = [
+        pltpu.make_async_copy(source, target, small_sems.at[j])
+        for j, (source, target) in enumerate(
+            (
+                (place_in, place_ref),
+                (span_in, span_ref),
+                (plen_in, plen_ref),
+                (dest_in, dest_ref),
+                (query_in, query_ref),
+            )
+        )
+    ]
+    for copy in small:
+        copy.start()
+    for copy in small:
+        copy.wait()
+    me = lax.axis_index("blk")
+    pieces = rows // PIECE
+
+    def bounds(token):
+        low = jnp.zeros_like(token)
+        pre_low = jnp.zeros_like(token)
+        pre_high = jnp.zeros_like(token) + plen_ref[0]
+        end = jnp.int32(0)
+        for r in range(requests - 1):
+            end = end + span_ref[r]
+            past = token >= end
+            low = low + jnp.where(past, span_ref[r], 0)
+            pre_low = pre_low + jnp.where(past, plen_ref[r], 0)
+            pre_high = pre_high + jnp.where(past, plen_ref[r + 1], 0)
+        return low, pre_low, pre_high
+
+    def tokens_of(index, shape, axis):
+        place = lax.broadcasted_iota(jnp.int32, shape, axis)
+        token = place
+        for piece in range(pieces):
+            start = place_ref[index * rows + piece * PIECE] - piece * PIECE
+            token = jnp.where(place >= piece * PIECE, place + start, token)
+        return token
+
+    token = tokens_of(me, (rows, rows), 0)
+    low, pre_low, pre_high = bounds(token)
+    column = lax.broadcasted_iota(jnp.int32, (rows, rows), 1)
+    earlier = jnp.where(lax.broadcasted_iota(jnp.int32, (rows, rows), 0) < column, 1.0, 0.0)
+    earlier = earlier.astype(jnp.bfloat16)
+    slot = lax.broadcasted_iota(jnp.int32, (capacity, rows), 0).astype(jnp.float32)
+    for n, offset in enumerate(offsets):
+        index = me ^ offset
+        position = column + index * rows
+        pre_seen = (position >= pre_low) & (position < pre_high)
+        key_token = tokens_of(index, (rows, rows), 1)
+        new_seen = (key_token >= low) & (key_token <= token)
+        bias_ref[n, :, :rows] = jnp.where(pre_seen, 0.0, LARGE_NEGATIVE).astype(jnp.float32)
+        bias_ref[n, :, rows:] = jnp.where(new_seen, 0.0, LARGE_NEGATIVE).astype(jnp.float32)
+        mine = jnp.where(dest_ref[pl.ds(index, 1), :] == me, 1.0, 0.0)
+        mine = jnp.broadcast_to(mine, (capacity, rows))
+        rank = dot_nn(mine.astype(jnp.bfloat16), earlier)
+        choose_ref[n] = jnp.where((rank == slot) & (mine > 0.5), 1.0, 0.0).astype(jnp.bfloat16)
+    copies = pick_rows(
+        (0,), [[own_ref]], [choose_ref.at[0]], (dkey_ref, dval_ref), picked_ref, sems
+    )
+    add_blocks(
+        [[own_ref]], [bias_ref.at[0]], query_ref, None, (max_ref, acc_ref), heads, groups, None
+    )
+    for copy in copies:
+        copy.wait()
+
+
+def stage_kernel(order, offsets, parts, last, heads, groups, *refs):
+    refs = list(refs)
+    query_ref, bias_ref, choose_ref = refs[:3]
+    refs = refs[3:]
+    blocks = []
+    for count in parts:
+        blocks.append(refs[:count])
+        refs = refs[count:]
+    before = refs[:2]
+    refs = refs[4:]
+    if last:
+        att_ref, dkey_ref, dval_ref, picked_ref, sems, att_vmem, att_sems = refs
+        after = None
+    else:
+        max_ref, acc_ref, dkey_ref, dval_ref, picked_ref, sems = refs
+        after = (max_ref, acc_ref)
+    copies = pick_rows(
+        offsets, blocks, [choose_ref.at[n] for n in order], (dkey_ref, dval_ref), picked_ref, sems
+    )
+
+    def store(k, g, result):
+        if g is not None:
+            att_vmem[:, (k * groups + g) * HD:(k * groups + g + 1) * HD] = result.astype(jnp.bfloat16)
+            return
+        columns = slice(k * groups * HD, (k + 1) * groups * HD)
+        copy = pltpu.make_async_copy(
+            att_vmem.at[:, columns], att_ref.at[:, columns], att_sems.at[k]
+        )
+        copy.start()
+        copies.append(copy)
+
+    add_blocks(
+        blocks, [bias_ref.at[n] for n in order], query_ref, before, after, heads, groups, store
+    )
+    for copy in copies:
+        copy.wait()
+
+
+def in_vmem(x):
+    return pltpu.with_memory_space_constraint(x, VMEM)
+
+
+def shapes_of(rows, columns, cycle):
+    groups = H // KVH
+    heads = columns // (groups * HD)
+    state = (
+        VMEM((heads, groups * rows, HD), jnp.float32),
+        VMEM((heads, groups * rows, 2 * HD), jnp.float32),
+    )
+    decode = jax.ShapeDtypeStruct((2 * rows, heads * HD), jnp.bfloat16)
+    return groups, heads, state, (decode, decode)
+
+
+def params(keys, rows, columns):
+    return dict(
+        compiler_params=pltpu.CompilerParams(vmem_limit_bytes=20 * 1024 * 1024),
+        cost_estimate=pl.CostEstimate(
+            flops=4 * rows * columns * keys, bytes_accessed=4 * 1024 * 1024, transcendentals=0
+        ),
+    )
+
+
+def run_first(small, query, own, offsets, capacity):
+    rows, columns = query.shape
+    cycle = len(offsets)
+    groups, heads, state, decode = shapes_of(rows, columns, cycle)
+    hbm, vmem = pl.BlockSpec(memory_space=HBM), pl.BlockSpec(memory_space=VMEM)
+    small = tuple(pltpu.with_memory_space_constraint(x, HBM) for x in small)
+    *state, dkey, dval, query, bias, choose = pl.pallas_call(
+        functools.partial(
+            first_kernel, offsets, rows, heads, groups, small[1].shape[0], capacity
+        ),
+        out_shape=(
+            *state,
+            *decode,
+            VMEM((rows, columns), jnp.bfloat16),
+            VMEM((cycle, rows, 2 * rows), jnp.float32),
+            VMEM((cycle, capacity, rows), jnp.bfloat16),
+        ),
+        in_specs=[hbm] * 5 + [vmem],
+        out_specs=(vmem, vmem, hbm, hbm, vmem, vmem, vmem),
+        scratch_shapes=[
+            *[SMEM(x.shape, jnp.int32) for x in small[:3]],
+            VMEM(small[3].shape, jnp.int32),
+            VMEM((1, 2, capacity, heads * HD), jnp.bfloat16),
+            pltpu.SemaphoreType.DMA((1, 2)),
+            pltpu.SemaphoreType.DMA((5,)),
+        ],
+        **params(2 * rows, rows, columns),
+    )(*small, pltpu.with_memory_space_constraint(query, HBM), in_vmem(own))
+    return [*state, dkey, dval], (query, bias, choose)
+
+
+def run_stage(common, order, offsets, blocks, carry, last):
+    rows, columns = common[0].shape
+    cycle, capacity, unused = common[2].shape
+    groups, heads, state, decode = shapes_of(rows, columns, cycle)
+    parts = tuple(len(block) for block in blocks)
+    flat = [in_vmem(ref) for block in blocks for ref in block]
+    hbm, vmem = pl.BlockSpec(memory_space=HBM), pl.BlockSpec(memory_space=VMEM)
+    operands = [*(in_vmem(x) for x in common), *flat]
+    at = len(operands)
+    operands += [in_vmem(carry[0]), in_vmem(carry[1]), *carry[2:]]
+    scratch = [
+        VMEM((len(blocks), 2, capacity, heads * HD), jnp.bfloat16),
+        pltpu.SemaphoreType.DMA((len(blocks), 2)),
+    ]
+    if last:
+        out_shape = (jax.ShapeDtypeStruct((rows, columns), jnp.bfloat16), *decode)
+        out_specs = (hbm, hbm, hbm)
+        alias = {at + 2: 1, at + 3: 2}
+        scratch += [VMEM((rows, columns), jnp.bfloat16), pltpu.SemaphoreType.DMA((heads,))]
+    else:
+        out_shape = (*state, *decode)
+        out_specs = (vmem, vmem, hbm, hbm)
+        alias = {at + j: j for j in range(4)}
+    return pl.pallas_call(
+        functools.partial(stage_kernel, order, offsets, parts, last, heads, groups),
+        out_shape=out_shape,
+        in_specs=[vmem] * (at + 2) + [hbm] * 2,
+        out_specs=out_specs,
+        input_output_aliases=alias,
+        scratch_shapes=scratch,
+        **params(2 * rows * len(blocks), rows, columns),
+    )(*operands)
+
+
+def pack_kernel(*refs):
+    *inputs, out_ref, sems = refs
+    rows = inputs[0].shape[0]
+    copies = [
+        pltpu.make_async_copy(ref, out_ref.at[j * rows:(j + 1) * rows], sems.at[j])
+        for j, ref in enumerate(inputs)
+    ]
+    for copy in copies:
+        copy.start()
+    for copy in copies:
+        copy.wait()
+
+
+def pack(*arrays):
+    rows, columns = arrays[0].shape
+    return pl.pallas_call(
+        pack_kernel,
+        out_shape=VMEM((rows * len(arrays), columns), jnp.bfloat16),
+        in_specs=[pl.BlockSpec(memory_space=HBM)] * len(arrays),
+        out_specs=pl.BlockSpec(memory_space=VMEM),
+        scratch_shapes=[pltpu.SemaphoreType.DMA((len(arrays),))],
+        compiler_params=pltpu.CompilerParams(vmem_limit_bytes=4 * 1024 * 1024),
+    )(*(pltpu.with_memory_space_constraint(x, HBM) for x in arrays))
+
+
+def choose_kernel(at_ends, between, *refs):
+    out_ref = refs[-1]
+    place = lax.axis_index("blk") // 2
+    outer = (place == 0) | (place == 3)
+
+    @pl.when(outer)
+    def _():
+        out_ref[...] = at_ends[...]
+
+    @pl.when(jnp.logical_not(outer))
+    def _():
+        out_ref[...] = between[...]
+
+
+def choose(at_ends, between, *after):
+    vmem = pl.BlockSpec(memory_space=VMEM)
+    return pl.pallas_call(
+        choose_kernel,
+        out_shape=VMEM(at_ends.shape, at_ends.dtype),
+        in_specs=[vmem] * (2 + len(after)),
+        out_specs=vmem,
+        compiler_params=pltpu.CompilerParams(vmem_limit_bytes=8 * 1024 * 1024),
+    )(in_vmem(at_ends), in_vmem(between), *(in_vmem(x) for x in after))
+
+
+def half_kernel(which, in_ref, *refs):
+    out_ref = refs[-1]
+    rows = out_ref.shape[0]
+    out_ref[...] = in_ref[which * rows:(which + 1) * rows]
+
+
+def half_of(x, which, *after):
+    vmem = pl.BlockSpec(memory_space=VMEM)
+    return pl.pallas_call(
+        functools.partial(half_kernel, which),
+        out_shape=VMEM((x.shape[0] // 2, x.shape[1]), x.dtype),
+        in_specs=[vmem] * (1 + len(after)),
+        out_specs=vmem,
+        compiler_params=pltpu.CompilerParams(vmem_limit_bytes=8 * 1024 * 1024),
+    )(in_vmem(x), *(in_vmem(y) for y in after))
+
+
+def together(values, *after):
+    return lax.optimization_barrier(tuple(values) + after)[: len(values)]
+
+
+def cycle_of_eight(
+    queries, new_keys, new_values, prefix_keys, prefix_values, span_lens, prefix_lens, placement, decode_dest
+):
+    cycle = lax.axis_size("blk")
+    rows = queries.shape[0]
+    capacity = 2 * rows // cycle
+
+    def moves(table):
+        return [(2 * a + y, 2 * b + y) for a, b in table.items() for y in range(2)]
+
+    swap = [(i, i ^ 1) for i in range(cycle)]
+    near = moves({0: 1, 1: 0, 2: 3, 3: 2})
+    middle = moves({1: 2, 2: 1})
+    ends = moves({0: 3, 3: 0})
+    skip = moves({0: 2, 3: 1, 2: 3, 1: 0})
+    send = lambda x, table: lax.ppermute(x, "blk", table)
+
+    small = (placement, span_lens, prefix_lens, decode_dest.reshape(cycle, rows))
+    own = pack(prefix_keys, prefix_values, new_keys, new_values)
+    half = own.shape[0] // 2
+
+    offsets = (0, 2, 1, 6, 3, 4, 7, 5)
+
+    a = send(own, near)
+    y_own = send(own, swap)
+    b_inner = send(own, middle)
+    carry, common = run_first(small, queries, own, offsets, capacity)
+
+    skip_from = choose(own, b_inner)
+    a_2, *carry = together((a, *carry))
+    y_a = send(a_2, swap)
+    own_2, *carry = together((choose(own, own, y_own), *carry))
+    b_outer = send(own_2, ends)
+    carry = run_stage(common, (1, 2), offsets[1:3], [[a_2], [y_own]], carry, False)
+
+    b = choose(b_outer, choose(b_inner, b_inner, y_a))
+    b, *carry = together((b, *carry))
+    y_b = send(b, swap)
+    skip_from, *carry = together((skip_from, *carry), b, y_a)
+    c = send(skip_from, skip)
+    carry = run_stage(common, (3, 4), offsets[3:5], [[b], [y_a]], carry, False)
+
+    y_b_high, *carry = together((half_of(y_b, 1), *carry))
+    y_c_high = send(y_b_high, near)
+    c_low, *carry = together((half_of(c, 0, y_b_high), *carry))
+    y_c_low = send(c_low, swap)
+    carry = run_stage(common, (5, 6), offsets[5:7], [[c], [y_b]], carry, False)
+    return tuple(run_stage(common, (7,), offsets[7:], [[y_c_low, y_c_high]], carry, True))
 
 
 masked_score = -1e30
@@ -84,7 +506,7 @@
     )
 
 
-def shards(
+def any_cycle(
     queries,
     new_keys,
     new_values,
@@ -171,25 +593,11 @@
 
 
 def solution(mesh):
-    placed = (
-        P(("groups", "blk"), "tensor"),
-        P(("groups", "blk"), "tensor"),
-        P(("groups", "blk"), "tensor"),
-        P(("groups", "blk"), "tensor"),
-        P(("groups", "blk"), "tensor"),
-        P("groups"),
-        P("groups"),
-        P("groups"),
-        P("groups", None),
-    )
+    rows = P(("groups", "blk"), "tensor")
     return jax.shard_map(
-        shards,
+        cycle_of_eight if mesh.shape["blk"] == 8 else any_cycle,
         mesh=mesh,
-        in_specs=placed,
-        out_specs=(
-            P(("groups", "blk"), "tensor"),
-            P(("groups", "blk"), "tensor"),
-            P(("groups", "blk"), "tensor"),
-        ),
+        in_specs=(rows,) * 5 + (P("groups"),) * 3 + (P("groups", None),),
+        out_specs=(rows,) * 3,
         check_vma=False,
     )

time: 221 us -> 58.8 us (0.27)
  waiting for transfers between devices: 111 us -> 22.2 us
  matrix products: 33.8 us -> 0 us
  other arithmetic: 29.3 us -> 0 us
  local copies, waits for them, and re-layouts: 22.6 us -> 0 us
  Pallas kernels: 0 us -> 20.4 us
  between operations: 15.1 us -> 0.92 us
  starting transfers between devices: 7.43 us -> 15.1 us
    all_gather x4 -> x0, waiting for transfers between devices: 99.3 us -> none  [the longest x1 41.1 us: shards(): piece_values = lax.all_gather(prefix_values, 'blk', axis=0, tiled=True)]
    dot_general x9 -> x0, matrix products: 33.8 us -> none  [the longest x4 19.9 us: one_block(): jnp.einsum('kgtn,nkd->kgtd', weights.astype(jnp.bfloat16), value_part, pr...]
    ppermute x0 -> x9, waiting for transfers between devices: none -> 22.2 us  [cycle_of_eight(): send = lambda x, table: lax.ppermute(x, 'blk', table)]
    pallas_call x0 -> x12, Pallas kernels: none -> 20.4 us  [the longest x4 15.6 us: run_stage(): pl.pallas_call(functools.partial(stage_kernel, order, offsets, parts, las...]
    ppermute x0 -> x9, starting transfers between devices: none -> 15.1 us  [cycle_of_eight(): send = lambda x, table: lax.ppermute(x, 'blk', table)]
    reduce_sum x8 -> x0, other arithmetic: 14.7 us -> none  [the longest x4 13.6 us: one_block(): running_sum = running_sum * rescale + jnp.sum(weights, axis=-1)]
    all_to_all x1 -> x0, waiting for transfers between devices: 9.37 us -> none  [shards(): lax.all_to_all(outgoing, 'blk', split_axis=0, concat_axis=0, tiled=True)]
    all_to_all x1 -> x0, starting transfers between devices: 7.28 us -> none  [shards(): lax.all_to_all(outgoing, 'blk', split_axis=0, concat_axis=0, tiled=True)]
  transfers between devices with their start and end apart: 5 -> 9, of which waited for: 5 -> 6; matrix products, arithmetic and copies ran while one was open for 24% -> 0% of each run, Pallas kernels for 0% -> 28%
where the time goes in v2:
time: 58.8 us; the launch traced here: 58.5 us
  waiting for transfers between devices  22.2 us (38%)
  Pallas kernels  20.4 us (35%)
  starting transfers between devices  15.1 us (26%)
  between operations  0.92 us (2%)
    ppermute x9, waiting for transfers between devices, cycle_of_eight(): send = lambda x, table: lax.ppermute(x, 'blk', table)  22.2 us
    pallas_call x4, Pallas kernels, run_stage(): pl.pallas_call(functools.partial(stage_kernel, order, offsets, parts, las...  15.6 us
    ppermute x9, starting transfers between devices, cycle_of_eight(): send = lambda x, table: lax.ppermute(x, 'blk', table)  15.1 us
    pallas_call x1, Pallas kernels, run_first(): pl.pallas_call(functools.partial(first_kernel, offsets, rows, heads, grou...  3.41 us
  transfers between devices with their start and end apart: 9, of which 6 were waited for; matrix products, arithmetic and copies ran while one was open for 0% of the time, Pallas kernels for 28%

profile of v2, /device:TPU:0, one launch (start us, length us, event | category | flops | bytes accessed | tf_op | source)
XLA Modules:
  0.0 58.5 jit_solution(17729275868544704576)
XLA Ops:
  0.6 1.1 %shard_map.112.own_ref.at_ends.between = bf16[512,512]{1,0:T(8,128)(2,1)S(1)} custom-call(bf16[128,512]{1,0:T(8,128)(2,1)} %refs_0_.1, bf16[128,512]{1,0:T(8,128)(2,1)} %refs_1_.1, bf16[128,512]{1,0:T(8,128)(2,1)} %refs_2_.1, bf16[128,512]{1,0:T(8,128)(2,1)} %refs_3_.1), custom_call_target="tpu_custom_call" | custom-call | tf_op jit(solution)/shard_map/pallas_call | solution.py:329
  1.8 3.1 %collective-permute-start.2 = (bf16[512,512]{1,0:T(8,128)(2,1)S(1)}, bf16[512,512]{1,0:T(8,128)(2,1)S(1)}, u32[]{:S(2)}, u32[]{:S(2)}) collective-permute-start(bf16[512,512]{1,0:T(8,128)(2,1)S(1)} %shard_map.112.own_ref.at_ends.between), channel_id=1, source_target_pairs={{0,4},{2,6},{4,0},{6,2},{8,12},{10,14},{12,8},{14,10},{1,5},{3,7},... | collective-permute-start | bytes 1572872 | tf_op jit(solution)/shard_map/ppermute | solution.py:400
  4.9 1.5 %collective-permute-start.1 = (bf16[512,512]{1,0:T(8,128)(2,1)S(1)}, bf16[512,512]{1,0:T(8,128)(2,1)S(1)}, u32[]{:S(2)}, u32[]{:S(2)}) collective-permute-start(bf16[512,512]{1,0:T(8,128)(2,1)S(1)} %shard_map.112.own_ref.at_ends.between), channel_id=1, source_target_pairs={{0,2},{2,0},{4,6},{6,4},{8,10},{10,8},{12,14},{14,12},{1,3},{3,1},... | collective-permute-start | bytes 1572872 | tf_op jit(solution)/shard_map/ppermute | solution.py:400
  6.4 0.7 %collective-permute-start = (bf16[512,512]{1,0:T(8,128)(2,1)S(1)}, bf16[512,512]{1,0:T(8,128)(2,1)S(1)}, u32[]{:S(2)}, u32[]{:S(2)}) collective-permute-start(bf16[512,512]{1,0:T(8,128)(2,1)S(1)} %shard_map.112.own_ref.at_ends.between), channel_id=1, source_target_pairs={{4,8},{6,10},{8,4},{10,6},{5,9},{7,11},{9,5},{11,7},{20,24},{22,26... | collective-permute-start | bytes 1572872 | tf_op jit(solution)/shard_map/ppermute | solution.py:400
  7.1 3.4 %shard_map.113 = (f32[4,1024,128]{2,1,0:T(8,128)S(1)}, f32[4,1024,256]{2,1,0:T(8,128)S(1)}, bf16[256,512]{1,0:T(8,128)(2,1)}, bf16[256,512]{1,0:T(8,128)(2,1)}, ...) custom-call(s32[1024]{0:T(1024)} %place_in.1, s32[2]{0:T(128)} %span_in.1, ...), custom_call_target="tpu_custom_call" | custom-call | flops 536870912 | bytes 4194304 | tf_op jit(solution)/shard_map/pallas_call | solution.py:255
  10.5 6.3 %collective-permute-done.2.refs_3_ = bf16[512,512]{1,0:T(8,128)(2,1)S(1)} collective-permute-done((bf16[512,512]{1,0:T(8,128)(2,1)S(1)}, bf16[512,512]{1,0:T(8,128)(2,1)S(1)}, u32[]{:S(2)}, u32[]{:S(2)}) %collective-permute-start.2) | collective-permute-done | bytes 524320 | tf_op jit(solution)/shard_map/ppermute | solution.py:400
  16.8 1.5 %collective-permute-done.1.refs_0_.refs_4_ = bf16[512,512]{1,0:T(8,128)(2,1)S(1)} collective-permute-done((bf16[512,512]{1,0:T(8,128)(2,1)S(1)}, bf16[512,512]{1,0:T(8,128)(2,1)S(1)}, u32[]{:S(2)}, u32[]{:S(2)}) %collective-permute-start.1) | collective-permute-done | bytes 524320 | tf_op jit(solution)/shard_map/ppermute | solution.py:400
  18.3 1.6 %collective-permute-start.4 = (bf16[512,512]{1,0:T(8,128)(2,1)S(1)}, bf16[512,512]{1,0:T(8,128)(2,1)S(1)}, u32[]{:S(2)}, u32[]{:S(2)}) collective-permute-start(bf16[512,512]{1,0:T(8,128)(2,1)S(1)} %collective-permute-done.2.refs_3_), channel_id=1, source_target_pairs={{0,2},{2,0},{4,6},{6,4},{8,10},{10,8},{12,14},{14,12},{1,3},{3,1},... | collective-permute-start | bytes 1572872 | tf_op jit(solution)/shard_map/ppermute | solution.py:400
  19.9 4.4 %collective-permute-start.3 = (bf16[512,512]{1,0:T(8,128)(2,1)S(1)}, bf16[512,512]{1,0:T(8,128)(2,1)S(1)}, u32[]{:S(2)}, u32[]{:S(2)}) collective-permute-start(bf16[512,512]{1,0:T(8,128)(2,1)S(1)} %shard_map.115), channel_id=1, source_target_pairs={{0,12},{2,14},{12,0},{14,2},{1,13},{3,15},{13,1},{15,3},{16,28},{1... | collective-permute-start | bytes 1572872 | tf_op jit(solution)/shard_map/ppermute | solution.py:400
  24.2 0.0 collective-permute-done.between.at_ends
  24.3 0.1 shard_map.114
  24.3 4.3 %shard_map.118 = (f32[4,1024,128]{2,1,0:T(8,128)S(1)}, f32[4,1024,256]{2,1,0:T(8,128)S(1)}, bf16[256,512]{1,0:T(8,128)(2,1)}, bf16[256,512]{1,0:T(8,128)(2,1)}) custom-call(bf16[128,4096]{1,0:T(8,128)(2,1)S(1)} %get-tuple-element.52.refs_0_, ...), custom_call_target="tpu_custom_call", output_to_operand_aliasing={{0}: (5, {}), {1}: (6, {}), {2}: (7, {}), {3}: (8, {})} | custom-call | flops 1073741824 | bytes 4194304 | tf_op jit(solution)/shard_map/pallas_call | solution.py:303
  28.7 2.1 %collective-permute-done.4.refs_0_.refs_4_ = bf16[512,512]{1,0:T(8,128)(2,1)S(1)} collective-permute-done((bf16[512,512]{1,0:T(8,128)(2,1)S(1)}, bf16[512,512]{1,0:T(8,128)(2,1)S(1)}, u32[]{:S(2)}, u32[]{:S(2)}) %collective-permute-start.4) | collective-permute-done | bytes 524320 | tf_op jit(solution)/shard_map/ppermute | solution.py:400
  30.9 4.9 %collective-permute-done.3.at_ends = bf16[512,512]{1,0:T(8,128)(2,1)S(1)} collective-permute-done((bf16[512,512]{1,0:T(8,128)(2,1)S(1)}, bf16[512,512]{1,0:T(8,128)(2,1)S(1)}, u32[]{:S(2)}, u32[]{:S(2)}) %collective-permute-start.3) | collective-permute-done | bytes 524320 | tf_op jit(solution)/shard_map/ppermute | solution.py:400
  35.8 0.6 collective-permute-start.6
  36.4 0.0 collective-permute-start.5
  36.4 4.3 %shard_map.120 = (f32[4,1024,128]{2,1,0:T(8,128)S(1)}, f32[4,1024,256]{2,1,0:T(8,128)S(1)}, bf16[256,512]{1,0:T(8,128)(2,1)}, bf16[256,512]{1,0:T(8,128)(2,1)}) custom-call(bf16[128,4096]{1,0:T(8,128)(2,1)S(1)} %get-tuple-element.52.refs_0_, ...), custom_call_target="tpu_custom_call", output_to_operand_aliasing={{0}: (5, {}), {1}: (6, {}), {2}: (7, {}), {3}: (8, {})} | custom-call | flops 1073741824 | bytes 4194304 | tf_op jit(solution)/shard_map/pallas_call | solution.py:303
  40.7 7.1 %collective-permute-done.6.in_ref.refs_4_ = bf16[512,512]{1,0:T(8,128)(2,1)S(1)} collective-permute-done((bf16[512,512]{1,0:T(8,128)(2,1)S(1)}, bf16[512,512]{1,0:T(8,128)(2,1)S(1)}, u32[]{:S(2)}, u32[]{:S(2)}) %collective-permute-start.6) | collective-permute-done | bytes 524320 | tf_op jit(solution)/shard_map/ppermute | solution.py:400
  47.8 0.0 collective-permute-done.5.in_ref.refs_3_
  47.9 1.5 %collective-permute-start.7 = (bf16[256,512]{1,0:T(8,128)(2,1)S(1)}, bf16[256,512]{1,0:T(8,128)(2,1)S(1)}, u32[]{:S(2)}, u32[]{:S(2)}) collective-permute-start(bf16[256,512]{1,0:T(8,128)(2,1)S(1)} %shard_map.121), channel_id=1, source_target_pairs={{0,2},{2,0},{4,6},{6,4},{8,10},{10,8},{12,14},{14,12},{1,3},{3,1},... | collective-permute-start | bytes 786440 | tf_op jit(solution)/shard_map/ppermute | solution.py:400
  49.4 1.7 %collective-permute-start.8 = (bf16[256,512]{1,0:T(8,128)(2,1)S(1)}, bf16[256,512]{1,0:T(8,128)(2,1)S(1)}, u32[]{:S(2)}, u32[]{:S(2)}) collective-permute-start(bf16[256,512]{1,0:T(8,128)(2,1)S(1)} %shard_map.119.refs_0_), channel_id=1, source_target_pairs={{0,4},{2,6},{4,0},{6,2},{8,12},{10,14},{12,8},{14,10},{1,5},{3,7},... | collective-permute-start | bytes 786440 | tf_op jit(solution)/shard_map/ppermute | solution.py:400
  51.1 4.3 %shard_map.122 = (f32[4,1024,128]{2,1,0:T(8,128)S(1)}, f32[4,1024,256]{2,1,0:T(8,128)S(1)}, bf16[256,512]{1,0:T(8,128)(2,1)}, bf16[256,512]{1,0:T(8,128)(2,1)}) custom-call(bf16[128,4096]{1,0:T(8,128)(2,1)S(1)} %get-tuple-element.52.refs_0_, ...), custom_call_target="tpu_custom_call", output_to_operand_aliasing={{0}: (5, {}), {1}: (6, {}), {2}: (7, {}), {3}: (8, {})} | custom-call | flops 1073741824 | bytes 4194304 | tf_op jit(solution)/shard_map/pallas_call | solution.py:303
  55.5 0.0 collective-permute-done.7.refs_3_
  55.5 0.3 collective-permute-done.8.refs_4_
  55.8 2.6 %shard_map.123 = (bf16[128,4096]{1,0:T(8,128)(2,1)}, bf16[256,512]{1,0:T(8,128)(2,1)}, bf16[256,512]{1,0:T(8,128)(2,1)}) custom-call(bf16[128,4096]{1,0:T(8,128)(2,1)S(1)} %get-tuple-element.52.refs_0_, f32[8,128,256]{2,1,0:T(8,128)S(1)} %get-tuple-element.53.refs_1_, ...), custom_call_target="tpu_custom_call", output_to_operand_aliasing={{1}: (7, {}), {2}: (8, {})} | custom-call | flops 536870912 | bytes 4194304 | tf_op jit(solution)/shard_map/pallas_call | solution.py:303
  (5 shorter events, 0.1 us)
Async XLA Ops:
  1.8 15.0 %collective-permute-start.2 = (bf16[512,512]{1,0:T(8,128)(2,1)S(1)}, bf16[512,512]{1,0:T(8,128)(2,1)S(1)}, u32[]{:S(2)}, u32[]{:S(2)}) collective-permute-start(bf16[512,512]{1,0:T(8,128)(2,1)S(1)} %shard_map.112.own_ref.at_ends.between), channel_id=1, source_target_pairs={{0,4},{2,6},{4,0},{6,2},{8,12},{10,14},{12,8},{14,10},{1,5},{3,7},... | collective-permute-start | bytes 1572872 | tf_op jit(solution)/shard_map/ppermute | solution.py:400
  4.9 13.4 %collective-permute-start.1 = (bf16[512,512]{1,0:T(8,128)(2,1)S(1)}, bf16[512,512]{1,0:T(8,128)(2,1)S(1)}, u32[]{:S(2)}, u32[]{:S(2)}) collective-permute-start(bf16[512,512]{1,0:T(8,128)(2,1)S(1)} %shard_map.112.own_ref.at_ends.between), channel_id=1, source_target_pairs={{0,2},{2,0},{4,6},{6,4},{8,10},{10,8},{12,14},{14,12},{1,3},{3,1},... | collective-permute-start | bytes 1572872 | tf_op jit(solution)/shard_map/ppermute | solution.py:400
  6.4 17.9 %collective-permute-start = (bf16[512,512]{1,0:T(8,128)(2,1)S(1)}, bf16[512,512]{1,0:T(8,128)(2,1)S(1)}, u32[]{:S(2)}, u32[]{:S(2)}) collective-permute-start(bf16[512,512]{1,0:T(8,128)(2,1)S(1)} %shard_map.112.own_ref.at_ends.between), channel_id=1, source_target_pairs={{4,8},{6,10},{8,4},{10,6},{5,9},{7,11},{9,5},{11,7},{20,24},{22,26... | collective-permute-start | bytes 1572872 | tf_op jit(solution)/shard_map/ppermute | solution.py:400
  18.3 12.5 %collective-permute-start.4 = (bf16[512,512]{1,0:T(8,128)(2,1)S(1)}, bf16[512,512]{1,0:T(8,128)(2,1)S(1)}, u32[]{:S(2)}, u32[]{:S(2)}) collective-permute-start(bf16[512,512]{1,0:T(8,128)(2,1)S(1)} %collective-permute-done.2.refs_3_), channel_id=1, source_target_pairs={{0,2},{2,0},{4,6},{6,4},{8,10},{10,8},{12,14},{14,12},{1,3},{3,1},... | collective-permute-start | bytes 1572872 | tf_op jit(solution)/shard_map/ppermute | solution.py:400
  19.9 15.9 %collective-permute-start.3 = (bf16[512,512]{1,0:T(8,128)(2,1)S(1)}, bf16[512,512]{1,0:T(8,128)(2,1)S(1)}, u32[]{:S(2)}, u32[]{:S(2)}) collective-permute-start(bf16[512,512]{1,0:T(8,128)(2,1)S(1)} %shard_map.115), channel_id=1, source_target_pairs={{0,12},{2,14},{12,0},{14,2},{1,13},{3,15},{13,1},{15,3},{16,28},{1... | collective-permute-start | bytes 1572872 | tf_op jit(solution)/shard_map/ppermute | solution.py:400
  35.8 12.0 %collective-permute-start.6 = (bf16[512,512]{1,0:T(8,128)(2,1)S(1)}, bf16[512,512]{1,0:T(8,128)(2,1)S(1)}, u32[]{:S(2)}, u32[]{:S(2)}) collective-permute-start(bf16[512,512]{1,0:T(8,128)(2,1)S(1)} %shard_map.117.refs_3_), channel_id=1, source_target_pairs={{0,2},{2,0},{4,6},{6,4},{8,10},{10,8},{12,14},{14,12},{1,3},{3,1},... | collective-permute-start | bytes 1572872 | tf_op jit(solution)/shard_map/ppermute | solution.py:400
  36.4 11.5 %collective-permute-start.5 = (bf16[512,512]{1,0:T(8,128)(2,1)S(1)}, bf16[512,512]{1,0:T(8,128)(2,1)S(1)}, u32[]{:S(2)}, u32[]{:S(2)}) collective-permute-start(bf16[512,512]{1,0:T(8,128)(2,1)S(1)} %shard_map.114), channel_id=1, source_target_pairs={{0,8},{2,10},{12,4},{14,6},{8,12},{10,14},{4,0},{6,2},{1,9},{3,11}... | collective-permute-start | bytes 1572872 | tf_op jit(solution)/shard_map/ppermute | solution.py:400
  47.9 7.6 %collective-permute-start.7 = (bf16[256,512]{1,0:T(8,128)(2,1)S(1)}, bf16[256,512]{1,0:T(8,128)(2,1)S(1)}, u32[]{:S(2)}, u32[]{:S(2)}) collective-permute-start(bf16[256,512]{1,0:T(8,128)(2,1)S(1)} %shard_map.121), channel_id=1, source_target_pairs={{0,2},{2,0},{4,6},{6,4},{8,10},{10,8},{12,14},{14,12},{1,3},{3,1},... | collective-permute-start | bytes 786440 | tf_op jit(solution)/shard_map/ppermute | solution.py:400
  49.4 6.4 %collective-permute-start.8 = (bf16[256,512]{1,0:T(8,128)(2,1)S(1)}, bf16[256,512]{1,0:T(8,128)(2,1)S(1)}, u32[]{:S(2)}, u32[]{:S(2)}) collective-permute-start(bf16[256,512]{1,0:T(8,128)(2,1)S(1)} %shard_map.119.refs_0_), channel_id=1, source_target_pairs={{0,4},{2,6},{4,0},{6,2},{8,12},{10,14},{12,8},{14,10},{1,5},{3,7},... | collective-permute-start | bytes 786440 | tf_op jit(solution)/shard_map/ppermute | solution.py:400

commit v3 on v2

--- a/solution.py
+++ b/solution.py
@@ -410,15 +410,15 @@
     b_inner = send(own, middle)
     carry, common = run_first(small, queries, own, offsets, capacity)
 
+    own_2, *carry = together((choose(own, own, a), *carry))
+    b_outer = send(own_2, ends)
+    a_2, *carry = together((choose(a, a, y_own, own_2), *carry))
+    y_a = send(a_2, swap)
+    carry = run_stage(common, (1, 2), offsets[1:3], [[a], [y_own]], carry, False)
+
     skip_from = choose(own, b_inner)
-    a_2, *carry = together((a, *carry))
-    y_a = send(a_2, swap)
-    own_2, *carry = together((choose(own, own, y_own), *carry))
-    b_outer = send(own_2, ends)
-    carry = run_stage(common, (1, 2), offsets[1:3], [[a_2], [y_own]], carry, False)
-
-    b = choose(b_outer, choose(b_inner, b_inner, y_a))
-    b, *carry = together((b, *carry))
+    b = choose(b_outer, b_inner)
+    b, *carry = together((choose(b, b, y_a), *carry))
     y_b = send(b, swap)
     skip_from, *carry = together((skip_from, *carry), b, y_a)
     c = send(skip_from, skip)

time: 58.8 us -> 58.2 us (0.990)
  waiting for transfers between devices: 22.2 us -> 21.2 us
    ppermute x9, waiting for transfers between devices: 22.2 us -> 21.2 us  [cycle_of_eight(): send = lambda x, table: lax.ppermute(x, 'blk', table)]
  transfers between devices with their start and end apart: 9 -> 9, of which waited for: 6 -> 7; matrix products, arithmetic and copies ran while one was open for 0% -> 0% of each run, Pallas kernels for 28% -> 29%
where the time goes in v3:
time: 58.2 us; the launch traced here: 58 us
  waiting for transfers between devices  21.2 us (36%)
  Pallas kernels  20.4 us (35%)
  starting transfers between devices  15.4 us (26%)
  between operations  0.91 us (2%)
    ppermute x9, waiting for transfers between devices, cycle_of_eight(): send = lambda x, table: lax.ppermute(x, 'blk', table)  21.2 us
    pallas_call x4, Pallas kernels, run_stage(): pl.pallas_call(functools.partial(stage_kernel, order, offsets, parts, las...  15.6 us
    ppermute x9, starting transfers between devices, cycle_of_eight(): send = lambda x, table: lax.ppermute(x, 'blk', table)  15.4 us
    pallas_call x1, Pallas kernels, run_first(): pl.pallas_call(functools.partial(first_kernel, offsets, rows, heads, grou...  3.41 us
  transfers between devices with their start and end apart: 9, of which 7 were waited for; matrix products, arithmetic and copies ran while one was open for 0% of the time, Pallas kernels for 29%

profile of v3, /device:TPU:0, one launch (start us, length us, event | category | flops | bytes accessed | tf_op | source)
XLA Modules:
  0.0 58.0 jit_solution(7610261378881452681)
XLA Ops:
  0.6 1.1 %shard_map.112.own_ref.at_ends.between = bf16[512,512]{1,0:T(8,128)(2,1)S(1)} custom-call(bf16[128,512]{1,0:T(8,128)(2,1)} %refs_0_.1, bf16[128,512]{1,0:T(8,128)(2,1)} %refs_1_.1, bf16[128,512]{1,0:T(8,128)(2,1)} %refs_2_.1, bf16[128,512]{1,0:T(8,128)(2,1)} %refs_3_.1), custom_call_target="tpu_custom_call" | custom-call | tf_op jit(solution)/shard_map/pallas_call | solution.py:329
  1.8 3.1 %collective-permute-start.1 = (bf16[512,512]{1,0:T(8,128)(2,1)S(1)}, bf16[512,512]{1,0:T(8,128)(2,1)S(1)}, u32[]{:S(2)}, u32[]{:S(2)}) collective-permute-start(bf16[512,512]{1,0:T(8,128)(2,1)S(1)} %shard_map.112.own_ref.at_ends.between), channel_id=1, source_target_pairs={{0,4},{2,6},{4,0},{6,2},{8,12},{10,14},{12,8},{14,10},{1,5},{3,7},... | collective-permute-start | bytes 1572872 | tf_op jit(solution)/shard_map/ppermute | solution.py:400
  4.9 1.5 %collective-permute-start.3 = (bf16[512,512]{1,0:T(8,128)(2,1)S(1)}, bf16[512,512]{1,0:T(8,128)(2,1)S(1)}, u32[]{:S(2)}, u32[]{:S(2)}) collective-permute-start(bf16[512,512]{1,0:T(8,128)(2,1)S(1)} %shard_map.112.own_ref.at_ends.between), channel_id=1, source_target_pairs={{0,2},{2,0},{4,6},{6,4},{8,10},{10,8},{12,14},{14,12},{1,3},{3,1},... | collective-permute-start | bytes 1572872 | tf_op jit(solution)/shard_map/ppermute | solution.py:400
  6.4 0.7 %collective-permute-start = (bf16[512,512]{1,0:T(8,128)(2,1)S(1)}, bf16[512,512]{1,0:T(8,128)(2,1)S(1)}, u32[]{:S(2)}, u32[]{:S(2)}) collective-permute-start(bf16[512,512]{1,0:T(8,128)(2,1)S(1)} %shard_map.112.own_ref.at_ends.between), channel_id=1, source_target_pairs={{4,8},{6,10},{8,4},{10,6},{5,9},{7,11},{9,5},{11,7},{20,24},{22,26... | collective-permute-start | bytes 1572872 | tf_op jit(solution)/shard_map/ppermute | solution.py:400
  7.1 3.4 %shard_map.113 = (f32[4,1024,128]{2,1,0:T(8,128)S(1)}, f32[4,1024,256]{2,1,0:T(8,128)S(1)}, bf16[256,512]{1,0:T(8,128)(2,1)}, bf16[256,512]{1,0:T(8,128)(2,1)}, ...) custom-call(s32[1024]{0:T(1024)} %place_in.1, s32[2]{0:T(128)} %span_in.1, ...), custom_call_target="tpu_custom_call" | custom-call | flops 536870912 | bytes 4194304 | tf_op jit(solution)/shard_map/pallas_call | solution.py:255
  10.5 6.3 %collective-permute-done.1.refs_0_.at_ends.between.refs_3_ = bf16[512,512]{1,0:T(8,128)(2,1)S(1)} collective-permute-done((bf16[512,512]{1,0:T(8,128)(2,1)S(1)}, bf16[512,512]{1,0:T(8,128)(2,1)S(1)}, u32[]{:S(2)}, u32[]{:S(2)}) %collective-permute-start.1) | collective-permute-done | bytes 524320 | tf_op jit(solution)/shard_map/ppermute | solution.py:400
  16.8 5.7 %collective-permute-start.2 = (bf16[512,512]{1,0:T(8,128)(2,1)S(1)}, bf16[512,512]{1,0:T(8,128)(2,1)S(1)}, u32[]{:S(2)}, u32[]{:S(2)}) collective-permute-start(bf16[512,512]{1,0:T(8,128)(2,1)S(1)} %shard_map.115.refs_1_), channel_id=1, source_target_pairs={{0,12},{2,14},{12,0},{14,2},{1,13},{3,15},{13,1},{15,3},{16,28},{1... | collective-permute-start | bytes 1572872 | tf_op jit(solution)/shard_map/ppermute | solution.py:400
  22.5 0.0 collective-permute-done.3.refs_0_.refs_4_
  22.5 0.1 shard_map.117
  22.6 1.6 %collective-permute-start.4 = (bf16[512,512]{1,0:T(8,128)(2,1)S(1)}, bf16[512,512]{1,0:T(8,128)(2,1)S(1)}, u32[]{:S(2)}, u32[]{:S(2)}) collective-permute-start(bf16[512,512]{1,0:T(8,128)(2,1)S(1)} %shard_map.117), channel_id=1, source_target_pairs={{0,2},{2,0},{4,6},{6,4},{8,10},{10,8},{12,14},{14,12},{1,3},{3,1},... | collective-permute-start | bytes 1572872 | tf_op jit(solution)/shard_map/ppermute | solution.py:400
  24.2 0.0 collective-permute-done.between
  24.2 4.3 %shard_map.119 = (f32[4,1024,128]{2,1,0:T(8,128)S(1)}, f32[4,1024,256]{2,1,0:T(8,128)S(1)}, bf16[256,512]{1,0:T(8,128)(2,1)}, bf16[256,512]{1,0:T(8,128)(2,1)}) custom-call(bf16[128,4096]{1,0:T(8,128)(2,1)S(1)} %get-tuple-element.52.refs_0_, ...), custom_call_target="tpu_custom_call", output_to_operand_aliasing={{0}: (5, {}), {1}: (6, {}), {2}: (7, {}), {3}: (8, {})} | custom-call | flops 1073741824 | bytes 4194304 | tf_op jit(solution)/shard_map/pallas_call | solution.py:303
  28.6 5.1 %collective-permute-done.2.at_ends = bf16[512,512]{1,0:T(8,128)(2,1)S(1)} collective-permute-done((bf16[512,512]{1,0:T(8,128)(2,1)S(1)}, bf16[512,512]{1,0:T(8,128)(2,1)S(1)}, u32[]{:S(2)}, u32[]{:S(2)}) %collective-permute-start.2) | collective-permute-done | bytes 524320 | tf_op jit(solution)/shard_map/ppermute | solution.py:400
  33.7 1.5 %collective-permute-done.4.refs_0_.refs_4_ = bf16[512,512]{1,0:T(8,128)(2,1)S(1)} collective-permute-done((bf16[512,512]{1,0:T(8,128)(2,1)S(1)}, bf16[512,512]{1,0:T(8,128)(2,1)S(1)}, u32[]{:S(2)}, u32[]{:S(2)}) %collective-permute-start.4) | collective-permute-done | bytes 524320 | tf_op jit(solution)/shard_map/ppermute | solution.py:400
  35.2 1.6 %collective-permute-start.6 = (bf16[512,512]{1,0:T(8,128)(2,1)S(1)}, bf16[512,512]{1,0:T(8,128)(2,1)S(1)}, u32[]{:S(2)}, u32[]{:S(2)}) collective-permute-start(bf16[512,512]{1,0:T(8,128)(2,1)S(1)} %shard_map.118.refs_3_), channel_id=1, source_target_pairs={{0,2},{2,0},{4,6},{6,4},{8,10},{10,8},{12,14},{14,12},{1,3},{3,1},... | collective-permute-start | bytes 1572872 | tf_op jit(solution)/shard_map/ppermute | solution.py:400
  36.8 0.0 collective-permute-start.5
  36.8 4.3 %shard_map.121 = (f32[4,1024,128]{2,1,0:T(8,128)S(1)}, f32[4,1024,256]{2,1,0:T(8,128)S(1)}, bf16[256,512]{1,0:T(8,128)(2,1)}, bf16[256,512]{1,0:T(8,128)(2,1)}) custom-call(bf16[128,4096]{1,0:T(8,128)(2,1)S(1)} %get-tuple-element.52.refs_0_, ...), custom_call_target="tpu_custom_call", output_to_operand_aliasing={{0}: (5, {}), {1}: (6, {}), {2}: (7, {}), {3}: (8, {})} | custom-call | flops 1073741824 | bytes 4194304 | tf_op jit(solution)/shard_map/pallas_call | solution.py:303
  41.1 5.7 %collective-permute-done.6.in_ref.refs_4_ = bf16[512,512]{1,0:T(8,128)(2,1)S(1)} collective-permute-done((bf16[512,512]{1,0:T(8,128)(2,1)S(1)}, bf16[512,512]{1,0:T(8,128)(2,1)S(1)}, u32[]{:S(2)}, u32[]{:S(2)}) %collective-permute-start.6) | collective-permute-done | bytes 524320 | tf_op jit(solution)/shard_map/ppermute | solution.py:400
  46.9 1.6 %collective-permute-done.5.in_ref.refs_3_ = bf16[512,512]{1,0:T(8,128)(2,1)S(1)} collective-permute-done((bf16[512,512]{1,0:T(8,128)(2,1)S(1)}, bf16[512,512]{1,0:T(8,128)(2,1)S(1)}, u32[]{:S(2)}, u32[]{:S(2)}) %collective-permute-start.5) | collective-permute-done | bytes 524320 | tf_op jit(solution)/shard_map/ppermute | solution.py:400
  48.5 0.4 collective-permute-start.7
  48.9 0.9 %collective-permute-start.8 = (bf16[256,512]{1,0:T(8,128)(2,1)S(1)}, bf16[256,512]{1,0:T(8,128)(2,1)S(1)}, u32[]{:S(2)}, u32[]{:S(2)}) collective-permute-start(bf16[256,512]{1,0:T(8,128)(2,1)S(1)} %shard_map.120.refs_0_), channel_id=1, source_target_pairs={{0,4},{2,6},{4,0},{6,2},{8,12},{10,14},{12,8},{14,10},{1,5},{3,7},... | collective-permute-start | bytes 786440 | tf_op jit(solution)/shard_map/ppermute | solution.py:400
  49.8 4.3 %shard_map.123 = (f32[4,1024,128]{2,1,0:T(8,128)S(1)}, f32[4,1024,256]{2,1,0:T(8,128)S(1)}, bf16[256,512]{1,0:T(8,128)(2,1)}, bf16[256,512]{1,0:T(8,128)(2,1)}) custom-call(bf16[128,4096]{1,0:T(8,128)(2,1)S(1)} %get-tuple-element.52.refs_0_, ...), custom_call_target="tpu_custom_call", output_to_operand_aliasing={{0}: (5, {}), {1}: (6, {}), {2}: (7, {}), {3}: (8, {})} | custom-call | flops 1073741824 | bytes 4194304 | tf_op jit(solution)/shard_map/pallas_call | solution.py:303
  54.2 0.8 %collective-permute-done.7.refs_3_ = bf16[256,512]{1,0:T(8,128)(2,1)S(1)} collective-permute-done((bf16[256,512]{1,0:T(8,128)(2,1)S(1)}, bf16[256,512]{1,0:T(8,128)(2,1)S(1)}, u32[]{:S(2)}, u32[]{:S(2)}) %collective-permute-start.7) | collective-permute-done | bytes 262176 | tf_op jit(solution)/shard_map/ppermute | solution.py:400
  54.9 0.3 collective-permute-done.8.refs_4_
  55.2 2.6 %shard_map.124 = (bf16[128,4096]{1,0:T(8,128)(2,1)}, bf16[256,512]{1,0:T(8,128)(2,1)}, bf16[256,512]{1,0:T(8,128)(2,1)}) custom-call(bf16[128,4096]{1,0:T(8,128)(2,1)S(1)} %get-tuple-element.52.refs_0_, f32[8,128,256]{2,1,0:T(8,128)S(1)} %get-tuple-element.53.refs_1_, ...), custom_call_target="tpu_custom_call", output_to_operand_aliasing={{1}: (7, {}), {2}: (8, {})} | custom-call | flops 536870912 | bytes 4194304 | tf_op jit(solution)/shard_map/pallas_call | solution.py:303
  (6 shorter events, 0.2 us)
Async XLA Ops:
  1.8 15.0 %collective-permute-start.1 = (bf16[512,512]{1,0:T(8,128)(2,1)S(1)}, bf16[512,512]{1,0:T(8,128)(2,1)S(1)}, u32[]{:S(2)}, u32[]{:S(2)}) collective-permute-start(bf16[512,512]{1,0:T(8,128)(2,1)S(1)} %shard_map.112.own_ref.at_ends.between), channel_id=1, source_target_pairs={{0,4},{2,6},{4,0},{6,2},{8,12},{10,14},{12,8},{14,10},{1,5},{3,7},... | collective-permute-start | bytes 1572872 | tf_op jit(solution)/shard_map/ppermute | solution.py:400
  4.9 17.7 %collective-permute-start.3 = (bf16[512,512]{1,0:T(8,128)(2,1)S(1)}, bf16[512,512]{1,0:T(8,128)(2,1)S(1)}, u32[]{:S(2)}, u32[]{:S(2)}) collective-permute-start(bf16[512,512]{1,0:T(8,128)(2,1)S(1)} %shard_map.112.own_ref.at_ends.between), channel_id=1, source_target_pairs={{0,2},{2,0},{4,6},{6,4},{8,10},{10,8},{12,14},{14,12},{1,3},{3,1},... | collective-permute-start | bytes 1572872 | tf_op jit(solution)/shard_map/ppermute | solution.py:400
  6.4 17.8 %collective-permute-start = (bf16[512,512]{1,0:T(8,128)(2,1)S(1)}, bf16[512,512]{1,0:T(8,128)(2,1)S(1)}, u32[]{:S(2)}, u32[]{:S(2)}) collective-permute-start(bf16[512,512]{1,0:T(8,128)(2,1)S(1)} %shard_map.112.own_ref.at_ends.between), channel_id=1, source_target_pairs={{4,8},{6,10},{8,4},{10,6},{5,9},{7,11},{9,5},{11,7},{20,24},{22,26... | collective-permute-start | bytes 1572872 | tf_op jit(solution)/shard_map/ppermute | solution.py:400
  16.8 16.8 %collective-permute-start.2 = (bf16[512,512]{1,0:T(8,128)(2,1)S(1)}, bf16[512,512]{1,0:T(8,128)(2,1)S(1)}, u32[]{:S(2)}, u32[]{:S(2)}) collective-permute-start(bf16[512,512]{1,0:T(8,128)(2,1)S(1)} %shard_map.115.refs_1_), channel_id=1, source_target_pairs={{0,12},{2,14},{12,0},{14,2},{1,13},{3,15},{13,1},{15,3},{16,28},{1... | collective-permute-start | bytes 1572872 | tf_op jit(solution)/shard_map/ppermute | solution.py:400
  22.6 12.6 %collective-permute-start.4 = (bf16[512,512]{1,0:T(8,128)(2,1)S(1)}, bf16[512,512]{1,0:T(8,128)(2,1)S(1)}, u32[]{:S(2)}, u32[]{:S(2)}) collective-permute-start(bf16[512,512]{1,0:T(8,128)(2,1)S(1)} %shard_map.117), channel_id=1, source_target_pairs={{0,2},{2,0},{4,6},{6,4},{8,10},{10,8},{12,14},{14,12},{1,3},{3,1},... | collective-permute-start | bytes 1572872 | tf_op jit(solution)/shard_map/ppermute | solution.py:400
  35.2 11.7 %collective-permute-start.6 = (bf16[512,512]{1,0:T(8,128)(2,1)S(1)}, bf16[512,512]{1,0:T(8,128)(2,1)S(1)}, u32[]{:S(2)}, u32[]{:S(2)}) collective-permute-start(bf16[512,512]{1,0:T(8,128)(2,1)S(1)} %shard_map.118.refs_3_), channel_id=1, source_target_pairs={{0,2},{2,0},{4,6},{6,4},{8,10},{10,8},{12,14},{14,12},{1,3},{3,1},... | collective-permute-start | bytes 1572872 | tf_op jit(solution)/shard_map/ppermute | solution.py:400
  36.8 11.7 %collective-permute-start.5 = (bf16[512,512]{1,0:T(8,128)(2,1)S(1)}, bf16[512,512]{1,0:T(8,128)(2,1)S(1)}, u32[]{:S(2)}, u32[]{:S(2)}) collective-permute-start(bf16[512,512]{1,0:T(8,128)(2,1)S(1)} %shard_map.114), channel_id=1, source_target_pairs={{0,8},{2,10},{12,4},{14,6},{8,12},{10,14},{4,0},{6,2},{1,9},{3,11}... | collective-permute-start | bytes 1572872 | tf_op jit(solution)/shard_map/ppermute | solution.py:400
  48.5 6.4 %collective-permute-start.7 = (bf16[256,512]{1,0:T(8,128)(2,1)S(1)}, bf16[256,512]{1,0:T(8,128)(2,1)S(1)}, u32[]{:S(2)}, u32[]{:S(2)}) collective-permute-start(bf16[256,512]{1,0:T(8,128)(2,1)S(1)} %shard_map.122), channel_id=1, source_target_pairs={{0,2},{2,0},{4,6},{6,4},{8,10},{10,8},{12,14},{14,12},{1,3},{3,1},... | collective-permute-start | bytes 786440 | tf_op jit(solution)/shard_map/ppermute | solution.py:400
  48.9 6.4 %collective-permute-start.8 = (bf16[256,512]{1,0:T(8,128)(2,1)S(1)}, bf16[256,512]{1,0:T(8,128)(2,1)S(1)}, u32[]{:S(2)}, u32[]{:S(2)}) collective-permute-start(bf16[256,512]{1,0:T(8,128)(2,1)S(1)} %shard_map.120.refs_0_), channel_id=1, source_target_pairs={{0,4},{2,6},{4,0},{6,2},{8,12},{10,14},{12,8},{14,10},{1,5},{3,7},... | collective-permute-start | bytes 786440 | tf_op jit(solution)/shard_map/ppermute | solution.py:400

commit v4 on v3

--- a/solution.py
+++ b/solution.py
@@ -416,18 +416,17 @@
     y_a = send(a_2, swap)
     carry = run_stage(common, (1, 2), offsets[1:3], [[a], [y_own]], carry, False)
 
-    skip_from = choose(own, b_inner)
-    b = choose(b_outer, b_inner)
-    b, *carry = together((choose(b, b, y_a), *carry))
+    skip_from, *carry = together((choose(own, b_inner, b_outer), *carry))
+    c = send(skip_from, skip)
+    b_outer, *carry = together((b_outer, *carry), skip_from)
+    b = choose(b_outer, b_inner, y_a)
     y_b = send(b, swap)
-    skip_from, *carry = together((skip_from, *carry), b, y_a)
-    c = send(skip_from, skip)
     carry = run_stage(common, (3, 4), offsets[3:5], [[b], [y_a]], carry, False)
 
-    y_b_high, *carry = together((half_of(y_b, 1), *carry))
+    c_low = half_of(c, 0, carry[0])
+    y_c_low = send(c_low, swap)
+    y_b_high, *carry = together((half_of(y_b, 1, c_low), *carry))
     y_c_high = send(y_b_high, near)
-    c_low, *carry = together((half_of(c, 0, y_b_high), *carry))
-    y_c_low = send(c_low, swap)
     carry = run_stage(common, (5, 6), offsets[5:7], [[c], [y_b]], carry, False)
     return tuple(run_stage(common, (7,), offsets[7:], [[y_c_low, y_c_high]], carry, True))
 

time: 58.2 us -> 57.4 us (0.986)
  waiting for transfers between devices: 21.2 us -> 19.1 us
  starting transfers between devices: 15.4 us -> 16.6 us
    ppermute x9, waiting for transfers between devices: 21.2 us -> 19.1 us  [cycle_of_eight(): send = lambda x, table: lax.ppermute(x, 'blk', table)]
    ppermute x9, starting transfers between devices: 15.4 us -> 16.6 us  [cycle_of_eight(): send = lambda x, table: lax.ppermute(x, 'blk', table)]
  transfers between devices with their start and end apart: 9 -> 9, of which waited for: 7 -> 6; matrix products, arithmetic and copies ran while one was open for 0% -> 0% of each run, Pallas kernels for 29% -> 29%
where the time goes in v4:
time: 57.4 us; the launch traced here: 57.2 us
  Pallas kernels  20.5 us (36%)
  waiting for transfers between devices  19.1 us (33%)
  starting transfers between devices  16.6 us (29%)
  between operations  0.92 us (2%)
    ppermute x9, waiting for transfers between devices, cycle_of_eight(): send = lambda x, table: lax.ppermute(x, 'blk', table)  19.1 us
    ppermute x9, starting transfers between devices, cycle_of_eight(): send = lambda x, table: lax.ppermute(x, 'blk', table)  16.6 us
    pallas_call x4, Pallas kernels, run_stage(): pl.pallas_call(functools.partial(stage_kernel, order, offsets, parts, las...  15.6 us
    pallas_call x1, Pallas kernels, run_first(): pl.pallas_call(functools.partial(first_kernel, offsets, rows, heads, grou...  3.41 us
  transfers between devices with their start and end apart: 9, of which 6 were waited for; matrix products, arithmetic and copies ran while one was open for 0% of the time, Pallas kernels for 29%

profile of v4, /device:TPU:0, one launch (start us, length us, event | category | flops | bytes accessed | tf_op | source)
XLA Modules:
  0.0 57.2 jit_solution(9889664212363086718)
XLA Ops:
  0.6 1.1 %shard_map.112.own_ref.at_ends.between = bf16[512,512]{1,0:T(8,128)(2,1)S(1)} custom-call(bf16[128,512]{1,0:T(8,128)(2,1)} %refs_0_.1, bf16[128,512]{1,0:T(8,128)(2,1)} %refs_1_.1, bf16[128,512]{1,0:T(8,128)(2,1)} %refs_2_.1, bf16[128,512]{1,0:T(8,128)(2,1)} %refs_3_.1), custom_call_target="tpu_custom_call" | custom-call | tf_op jit(solution)/shard_map/pallas_call | solution.py:329
  1.8 3.1 %collective-permute-start.1 = (bf16[512,512]{1,0:T(8,128)(2,1)S(1)}, bf16[512,512]{1,0:T(8,128)(2,1)S(1)}, u32[]{:S(2)}, u32[]{:S(2)}) collective-permute-start(bf16[512,512]{1,0:T(8,128)(2,1)S(1)} %shard_map.112.own_ref.at_ends.between), channel_id=1, source_target_pairs={{0,4},{2,6},{4,0},{6,2},{8,12},{10,14},{12,8},{14,10},{1,5},{3,7},... | collective-permute-start | bytes 1572872 | tf_op jit(solution)/shard_map/ppermute | solution.py:400
  4.9 1.5 %collective-permute-start.3 = (bf16[512,512]{1,0:T(8,128)(2,1)S(1)}, bf16[512,512]{1,0:T(8,128)(2,1)S(1)}, u32[]{:S(2)}, u32[]{:S(2)}) collective-permute-start(bf16[512,512]{1,0:T(8,128)(2,1)S(1)} %shard_map.112.own_ref.at_ends.between), channel_id=1, source_target_pairs={{0,2},{2,0},{4,6},{6,4},{8,10},{10,8},{12,14},{14,12},{1,3},{3,1},... | collective-permute-start | bytes 1572872 | tf_op jit(solution)/shard_map/ppermute | solution.py:400
  6.4 0.7 %collective-permute-start = (bf16[512,512]{1,0:T(8,128)(2,1)S(1)}, bf16[512,512]{1,0:T(8,128)(2,1)S(1)}, u32[]{:S(2)}, u32[]{:S(2)}) collective-permute-start(bf16[512,512]{1,0:T(8,128)(2,1)S(1)} %shard_map.112.own_ref.at_ends.between), channel_id=1, source_target_pairs={{4,8},{6,10},{8,4},{10,6},{5,9},{7,11},{9,5},{11,7},{20,24},{22,26... | collective-permute-start | bytes 1572872 | tf_op jit(solution)/shard_map/ppermute | solution.py:400
  7.1 3.4 %shard_map.113 = (f32[4,1024,128]{2,1,0:T(8,128)S(1)}, f32[4,1024,256]{2,1,0:T(8,128)S(1)}, bf16[256,512]{1,0:T(8,128)(2,1)}, bf16[256,512]{1,0:T(8,128)(2,1)}, ...) custom-call(s32[1024]{0:T(1024)} %place_in.1, s32[2]{0:T(128)} %span_in.1, ...), custom_call_target="tpu_custom_call" | custom-call | flops 536870912 | bytes 4194304 | tf_op jit(solution)/shard_map/pallas_call | solution.py:255
  10.5 6.3 %collective-permute-done.1.refs_0_.at_ends.between.refs_3_ = bf16[512,512]{1,0:T(8,128)(2,1)S(1)} collective-permute-done((bf16[512,512]{1,0:T(8,128)(2,1)S(1)}, bf16[512,512]{1,0:T(8,128)(2,1)S(1)}, u32[]{:S(2)}, u32[]{:S(2)}) %collective-permute-start.1) | collective-permute-done | bytes 524320 | tf_op jit(solution)/shard_map/ppermute | solution.py:400
  16.8 5.7 %collective-permute-start.2 = (bf16[512,512]{1,0:T(8,128)(2,1)S(1)}, bf16[512,512]{1,0:T(8,128)(2,1)S(1)}, u32[]{:S(2)}, u32[]{:S(2)}) collective-permute-start(bf16[512,512]{1,0:T(8,128)(2,1)S(1)} %shard_map.114.refs_1_), channel_id=1, source_target_pairs={{0,12},{2,14},{12,0},{14,2},{1,13},{3,15},{13,1},{15,3},{16,28},{1... | collective-permute-start | bytes 1572872 | tf_op jit(solution)/shard_map/ppermute | solution.py:400
  22.5 0.0 collective-permute-done.3.refs_0_.refs_4_
  22.5 0.1 shard_map.116
  22.6 1.6 %collective-permute-start.5 = (bf16[512,512]{1,0:T(8,128)(2,1)S(1)}, bf16[512,512]{1,0:T(8,128)(2,1)S(1)}, u32[]{:S(2)}, u32[]{:S(2)}) collective-permute-start(bf16[512,512]{1,0:T(8,128)(2,1)S(1)} %shard_map.116), channel_id=1, source_target_pairs={{0,2},{2,0},{4,6},{6,4},{8,10},{10,8},{12,14},{14,12},{1,3},{3,1},... | collective-permute-start | bytes 1572872 | tf_op jit(solution)/shard_map/ppermute | solution.py:400
  24.2 4.3 %shard_map.117 = (f32[4,1024,128]{2,1,0:T(8,128)S(1)}, f32[4,1024,256]{2,1,0:T(8,128)S(1)}, bf16[256,512]{1,0:T(8,128)(2,1)}, bf16[256,512]{1,0:T(8,128)(2,1)}) custom-call(bf16[128,4096]{1,0:T(8,128)(2,1)S(1)} %get-tuple-element.47.refs_0_, ...), custom_call_target="tpu_custom_call", output_to_operand_aliasing={{0}: (5, {}), {1}: (6, {}), {2}: (7, {}), {3}: (8, {})} | custom-call | flops 1073741824 | bytes 4194304 | tf_op jit(solution)/shard_map/pallas_call | solution.py:303
  28.5 0.0 collective-permute-done.between
  28.5 5.1 %collective-permute-done.2.refs_0_.at_ends = bf16[512,512]{1,0:T(8,128)(2,1)S(1)} collective-permute-done((bf16[512,512]{1,0:T(8,128)(2,1)S(1)}, bf16[512,512]{1,0:T(8,128)(2,1)S(1)}, u32[]{:S(2)}, u32[]{:S(2)}) %collective-permute-start.2) | collective-permute-done | bytes 524320 | tf_op jit(solution)/shard_map/ppermute | solution.py:400
  33.7 0.1 collective-permute-start.4
  33.7 1.4 %collective-permute-done.5.refs_0_.refs_4_ = bf16[512,512]{1,0:T(8,128)(2,1)S(1)} collective-permute-done((bf16[512,512]{1,0:T(8,128)(2,1)S(1)}, bf16[512,512]{1,0:T(8,128)(2,1)S(1)}, u32[]{:S(2)}, u32[]{:S(2)}) %collective-permute-start.5) | collective-permute-done | bytes 524320 | tf_op jit(solution)/shard_map/ppermute | solution.py:400
  35.2 0.2 shard_map.118.refs_3_
  35.4 1.6 %collective-permute-start.7 = (bf16[512,512]{1,0:T(8,128)(2,1)S(1)}, bf16[512,512]{1,0:T(8,128)(2,1)S(1)}, u32[]{:S(2)}, u32[]{:S(2)}) collective-permute-start(bf16[512,512]{1,0:T(8,128)(2,1)S(1)} %shard_map.118.refs_3_), channel_id=1, source_target_pairs={{0,2},{2,0},{4,6},{6,4},{8,10},{10,8},{12,14},{14,12},{1,3},{3,1},... | collective-permute-start | bytes 1572872 | tf_op jit(solution)/shard_map/ppermute | solution.py:400
  37.0 4.3 %shard_map.119 = (f32[4,1024,128]{2,1,0:T(8,128)S(1)}, f32[4,1024,256]{2,1,0:T(8,128)S(1)}, bf16[256,512]{1,0:T(8,128)(2,1)}, bf16[256,512]{1,0:T(8,128)(2,1)}) custom-call(bf16[128,4096]{1,0:T(8,128)(2,1)S(1)} %get-tuple-element.47.refs_0_, ...), custom_call_target="tpu_custom_call", output_to_operand_aliasing={{0}: (5, {}), {1}: (6, {}), {2}: (7, {}), {3}: (8, {})} | custom-call | flops 1073741824 | bytes 4194304 | tf_op jit(solution)/shard_map/pallas_call | solution.py:303
  41.3 4.6 %collective-permute-done.4.in_ref.refs_3_ = bf16[512,512]{1,0:T(8,128)(2,1)S(1)} collective-permute-done((bf16[512,512]{1,0:T(8,128)(2,1)S(1)}, bf16[512,512]{1,0:T(8,128)(2,1)S(1)}, u32[]{:S(2)}, u32[]{:S(2)}) %collective-permute-start.4) | collective-permute-done | bytes 524320 | tf_op jit(solution)/shard_map/ppermute | solution.py:400
  45.9 1.1 %collective-permute-done.7.in_ref.refs_4_ = bf16[512,512]{1,0:T(8,128)(2,1)S(1)} collective-permute-done((bf16[512,512]{1,0:T(8,128)(2,1)S(1)}, bf16[512,512]{1,0:T(8,128)(2,1)S(1)}, u32[]{:S(2)}, u32[]{:S(2)}) %collective-permute-start.7) | collective-permute-done | bytes 524320 | tf_op jit(solution)/shard_map/ppermute | solution.py:400
  47.1 1.0 %collective-permute-start.8 = (bf16[256,512]{1,0:T(8,128)(2,1)S(1)}, bf16[256,512]{1,0:T(8,128)(2,1)S(1)}, u32[]{:S(2)}, u32[]{:S(2)}) collective-permute-start(bf16[256,512]{1,0:T(8,128)(2,1)S(1)} %shard_map.121), channel_id=1, source_target_pairs={{0,4},{2,6},{4,0},{6,2},{8,12},{10,14},{12,8},{14,10},{1,5},{3,7},... | collective-permute-start | bytes 786440 | tf_op jit(solution)/shard_map/ppermute | solution.py:400
  48.0 1.5 %collective-permute-start.6 = (bf16[256,512]{1,0:T(8,128)(2,1)S(1)}, bf16[256,512]{1,0:T(8,128)(2,1)S(1)}, u32[]{:S(2)}, u32[]{:S(2)}) collective-permute-start(bf16[256,512]{1,0:T(8,128)(2,1)S(1)} %shard_map.120.refs_0_), channel_id=1, source_target_pairs={{0,2},{2,0},{4,6},{6,4},{8,10},{10,8},{12,14},{14,12},{1,3},{3,1},... | collective-permute-start | bytes 786440 | tf_op jit(solution)/shard_map/ppermute | solution.py:400
  49.5 4.3 %shard_map.122 = (f32[4,1024,128]{2,1,0:T(8,128)S(1)}, f32[4,1024,256]{2,1,0:T(8,128)S(1)}, bf16[256,512]{1,0:T(8,128)(2,1)}, bf16[256,512]{1,0:T(8,128)(2,1)}) custom-call(bf16[128,4096]{1,0:T(8,128)(2,1)S(1)} %get-tuple-element.47.refs_0_, ...), custom_call_target="tpu_custom_call", output_to_operand_aliasing={{0}: (5, {}), {1}: (6, {}), {2}: (7, {}), {3}: (8, {})} | custom-call | flops 1073741824 | bytes 4194304 | tf_op jit(solution)/shard_map/pallas_call | solution.py:303
  53.9 0.0 collective-permute-done.8.refs_4_
  53.9 0.5 collective-permute-done.6.refs_3_
  54.4 2.6 %shard_map.123 = (bf16[128,4096]{1,0:T(8,128)(2,1)}, bf16[256,512]{1,0:T(8,128)(2,1)}, bf16[256,512]{1,0:T(8,128)(2,1)}) custom-call(bf16[128,4096]{1,0:T(8,128)(2,1)S(1)} %get-tuple-element.47.refs_0_, f32[8,128,256]{2,1,0:T(8,128)S(1)} %get-tuple-element.48.refs_1_, ...), custom_call_target="tpu_custom_call", output_to_operand_aliasing={{1}: (7, {}), {2}: (8, {})} | custom-call | flops 536870912 | bytes 4194304 | tf_op jit(solution)/shard_map/pallas_call | solution.py:303
  (4 shorter events, 0.1 us)
Async XLA Ops:
  1.8 15.0 %collective-permute-start.1 = (bf16[512,512]{1,0:T(8,128)(2,1)S(1)}, bf16[512,512]{1,0:T(8,128)(2,1)S(1)}, u32[]{:S(2)}, u32[]{:S(2)}) collective-permute-start(bf16[512,512]{1,0:T(8,128)(2,1)S(1)} %shard_map.112.own_ref.at_ends.between), channel_id=1, source_target_pairs={{0,4},{2,6},{4,0},{6,2},{8,12},{10,14},{12,8},{14,10},{1,5},{3,7},... | collective-permute-start | bytes 1572872 | tf_op jit(solution)/shard_map/ppermute | solution.py:400
  4.9 17.7 %collective-permute-start.3 = (bf16[512,512]{1,0:T(8,128)(2,1)S(1)}, bf16[512,512]{1,0:T(8,128)(2,1)S(1)}, u32[]{:S(2)}, u32[]{:S(2)}) collective-permute-start(bf16[512,512]{1,0:T(8,128)(2,1)S(1)} %shard_map.112.own_ref.at_ends.between), channel_id=1, source_target_pairs={{0,2},{2,0},{4,6},{6,4},{8,10},{10,8},{12,14},{14,12},{1,3},{3,1},... | collective-permute-start | bytes 1572872 | tf_op jit(solution)/shard_map/ppermute | solution.py:400
  6.4 22.1 %collective-permute-start = (bf16[512,512]{1,0:T(8,128)(2,1)S(1)}, bf16[512,512]{1,0:T(8,128)(2,1)S(1)}, u32[]{:S(2)}, u32[]{:S(2)}) collective-permute-start(bf16[512,512]{1,0:T(8,128)(2,1)S(1)} %shard_map.112.own_ref.at_ends.between), channel_id=1, source_target_pairs={{4,8},{6,10},{8,4},{10,6},{5,9},{7,11},{9,5},{11,7},{20,24},{22,26... | collective-permute-start | bytes 1572872 | tf_op jit(solution)/shard_map/ppermute | solution.py:400
  16.8 16.8 %collective-permute-start.2 = (bf16[512,512]{1,0:T(8,128)(2,1)S(1)}, bf16[512,512]{1,0:T(8,128)(2,1)S(1)}, u32[]{:S(2)}, u32[]{:S(2)}) collective-permute-start(bf16[512,512]{1,0:T(8,128)(2,1)S(1)} %shard_map.114.refs_1_), channel_id=1, source_target_pairs={{0,12},{2,14},{12,0},{14,2},{1,13},{3,15},{13,1},{15,3},{16,28},{1... | collective-permute-start | bytes 1572872 | tf_op jit(solution)/shard_map/ppermute | solution.py:400
  22.6 12.6 %collective-permute-start.5 = (bf16[512,512]{1,0:T(8,128)(2,1)S(1)}, bf16[512,512]{1,0:T(8,128)(2,1)S(1)}, u32[]{:S(2)}, u32[]{:S(2)}) collective-permute-start(bf16[512,512]{1,0:T(8,128)(2,1)S(1)} %shard_map.116), channel_id=1, source_target_pairs={{0,2},{2,0},{4,6},{6,4},{8,10},{10,8},{12,14},{14,12},{1,3},{3,1},... | collective-permute-start | bytes 1572872 | tf_op jit(solution)/shard_map/ppermute | solution.py:400
  33.7 12.2 %collective-permute-start.4 = (bf16[512,512]{1,0:T(8,128)(2,1)S(1)}, bf16[512,512]{1,0:T(8,128)(2,1)S(1)}, u32[]{:S(2)}, u32[]{:S(2)}) collective-permute-start(bf16[512,512]{1,0:T(8,128)(2,1)S(1)} %shard_map.115), channel_id=1, source_target_pairs={{0,8},{2,10},{12,4},{14,6},{8,12},{10,14},{4,0},{6,2},{1,9},{3,11}... | collective-permute-start | bytes 1572872 | tf_op jit(solution)/shard_map/ppermute | solution.py:400
  35.4 11.7 %collective-permute-start.7 = (bf16[512,512]{1,0:T(8,128)(2,1)S(1)}, bf16[512,512]{1,0:T(8,128)(2,1)S(1)}, u32[]{:S(2)}, u32[]{:S(2)}) collective-permute-start(bf16[512,512]{1,0:T(8,128)(2,1)S(1)} %shard_map.118.refs_3_), channel_id=1, source_target_pairs={{0,2},{2,0},{4,6},{6,4},{8,10},{10,8},{12,14},{14,12},{1,3},{3,1},... | collective-permute-start | bytes 1572872 | tf_op jit(solution)/shard_map/ppermute | solution.py:400
  47.1 6.8 %collective-permute-start.8 = (bf16[256,512]{1,0:T(8,128)(2,1)S(1)}, bf16[256,512]{1,0:T(8,128)(2,1)S(1)}, u32[]{:S(2)}, u32[]{:S(2)}) collective-permute-start(bf16[256,512]{1,0:T(8,128)(2,1)S(1)} %shard_map.121), channel_id=1, source_target_pairs={{0,4},{2,6},{4,0},{6,2},{8,12},{10,14},{12,8},{14,10},{1,5},{3,7},... | collective-permute-start | bytes 786440 | tf_op jit(solution)/shard_map/ppermute | solution.py:400
  48.0 6.4 %collective-permute-start.6 = (bf16[256,512]{1,0:T(8,128)(2,1)S(1)}, bf16[256,512]{1,0:T(8,128)(2,1)S(1)}, u32[]{:S(2)}, u32[]{:S(2)}) collective-permute-start(bf16[256,512]{1,0:T(8,128)(2,1)S(1)} %shard_map.120.refs_0_), channel_id=1, source_target_pairs={{0,2},{2,0},{4,6},{6,4},{8,10},{10,8},{12,14},{14,12},{1,3},{3,1},... | collective-permute-start | bytes 786440 | tf_op jit(solution)/shard_map/ppermute | solution.py:400

commit v5 on v4

--- a/solution.py
+++ b/solution.py
@@ -428,7 +428,7 @@
     y_b_high, *carry = together((half_of(y_b, 1, c_low), *carry))
     y_c_high = send(y_b_high, near)
     carry = run_stage(common, (5, 6), offsets[5:7], [[c], [y_b]], carry, False)
-    return tuple(run_stage(common, (7,), offsets[7:], [[y_c_low, y_c_high]], carry, True))
+    return tuple(run_stage(common, (7,), offsets[7:], [[choose(y_c_low, y_c_low), y_c_high]], carry, True))
 
 
 masked_score = -1e30

time: 57.4 us -> 57.4 us (level)
  no operation moved by 1% of the time
where the time goes in v5:
time: 57.4 us; the launch traced here: 57.2 us
  Pallas kernels  20.6 us (36%)
  waiting for transfers between devices  18.7 us (33%)
  starting transfers between devices  17 us (30%)
  between operations  0.93 us (2%)
    ppermute x9, waiting for transfers between devices, cycle_of_eight(): send = lambda x, table: lax.ppermute(x, 'blk', table)  18.7 us
    ppermute x9, starting transfers between devices, cycle_of_eight(): send = lambda x, table: lax.ppermute(x, 'blk', table)  17 us
    pallas_call x4, Pallas kernels, run_stage(): pl.pallas_call(functools.partial(stage_kernel, order, offsets, parts, las...  15.6 us
    pallas_call x1, Pallas kernels, run_first(): pl.pallas_call(functools.partial(first_kernel, offsets, rows, heads, grou...  3.41 us
  transfers between devices with their start and end apart: 9, of which 6 were waited for; matrix products, arithmetic and copies ran while one was open for 0% of the time, Pallas kernels for 29%

profile of v5, /device:TPU:0, one launch (start us, length us, event | category | flops | bytes accessed | tf_op | source)
XLA Modules:
  0.0 57.2 jit_solution(10052794106775690747)
XLA Ops:
  0.6 1.1 %shard_map.112.own_ref.at_ends.between = bf16[512,512]{1,0:T(8,128)(2,1)S(1)} custom-call(bf16[128,512]{1,0:T(8,128)(2,1)} %refs_0_.1, bf16[128,512]{1,0:T(8,128)(2,1)} %refs_1_.1, bf16[128,512]{1,0:T(8,128)(2,1)} %refs_2_.1, bf16[128,512]{1,0:T(8,128)(2,1)} %refs_3_.1), custom_call_target="tpu_custom_call" | custom-call | tf_op jit(solution)/shard_map/pallas_call | solution.py:329
  1.8 3.1 %collective-permute-start.1 = (bf16[512,512]{1,0:T(8,128)(2,1)S(1)}, bf16[512,512]{1,0:T(8,128)(2,1)S(1)}, u32[]{:S(2)}, u32[]{:S(2)}) collective-permute-start(bf16[512,512]{1,0:T(8,128)(2,1)S(1)} %shard_map.112.own_ref.at_ends.between), channel_id=1, source_target_pairs={{0,4},{2,6},{4,0},{6,2},{8,12},{10,14},{12,8},{14,10},{1,5},{3,7},... | collective-permute-start | bytes 1572872 | tf_op jit(solution)/shard_map/ppermute | solution.py:400
  4.9 1.5 %collective-permute-start.3 = (bf16[512,512]{1,0:T(8,128)(2,1)S(1)}, bf16[512,512]{1,0:T(8,128)(2,1)S(1)}, u32[]{:S(2)}, u32[]{:S(2)}) collective-permute-start(bf16[512,512]{1,0:T(8,128)(2,1)S(1)} %shard_map.112.own_ref.at_ends.between), channel_id=1, source_target_pairs={{0,2},{2,0},{4,6},{6,4},{8,10},{10,8},{12,14},{14,12},{1,3},{3,1},... | collective-permute-start | bytes 1572872 | tf_op jit(solution)/shard_map/ppermute | solution.py:400
  6.4 0.7 %collective-permute-start = (bf16[512,512]{1,0:T(8,128)(2,1)S(1)}, bf16[512,512]{1,0:T(8,128)(2,1)S(1)}, u32[]{:S(2)}, u32[]{:S(2)}) collective-permute-start(bf16[512,512]{1,0:T(8,128)(2,1)S(1)} %shard_map.112.own_ref.at_ends.between), channel_id=1, source_target_pairs={{4,8},{6,10},{8,4},{10,6},{5,9},{7,11},{9,5},{11,7},{20,24},{22,26... | collective-permute-start | bytes 1572872 | tf_op jit(solution)/shard_map/ppermute | solution.py:400
  7.1 3.4 %shard_map.113 = (f32[4,1024,128]{2,1,0:T(8,128)S(1)}, f32[4,1024,256]{2,1,0:T(8,128)S(1)}, bf16[256,512]{1,0:T(8,128)(2,1)}, bf16[256,512]{1,0:T(8,128)(2,1)}, ...) custom-call(s32[1024]{0:T(1024)} %place_in.1, s32[2]{0:T(128)} %span_in.1, ...), custom_call_target="tpu_custom_call" | custom-call | flops 536870912 | bytes 4194304 | tf_op jit(solution)/shard_map/pallas_call | solution.py:255
  10.5 6.3 %collective-permute-done.1.refs_0_.at_ends.between.refs_3_ = bf16[512,512]{1,0:T(8,128)(2,1)S(1)} collective-permute-done((bf16[512,512]{1,0:T(8,128)(2,1)S(1)}, bf16[512,512]{1,0:T(8,128)(2,1)S(1)}, u32[]{:S(2)}, u32[]{:S(2)}) %collective-permute-start.1) | collective-permute-done | bytes 524320 | tf_op jit(solution)/shard_map/ppermute | solution.py:400
  16.8 5.7 %collective-permute-start.2 = (bf16[512,512]{1,0:T(8,128)(2,1)S(1)}, bf16[512,512]{1,0:T(8,128)(2,1)S(1)}, u32[]{:S(2)}, u32[]{:S(2)}) collective-permute-start(bf16[512,512]{1,0:T(8,128)(2,1)S(1)} %shard_map.114.refs_1_), channel_id=1, source_target_pairs={{0,12},{2,14},{12,0},{14,2},{1,13},{3,15},{13,1},{15,3},{16,28},{1... | collective-permute-start | bytes 1572872 | tf_op jit(solution)/shard_map/ppermute | solution.py:400
  22.5 0.0 collective-permute-done.3.refs_0_.refs_4_
  22.5 0.1 shard_map.116
  22.6 1.6 %collective-permute-start.5 = (bf16[512,512]{1,0:T(8,128)(2,1)S(1)}, bf16[512,512]{1,0:T(8,128)(2,1)S(1)}, u32[]{:S(2)}, u32[]{:S(2)}) collective-permute-start(bf16[512,512]{1,0:T(8,128)(2,1)S(1)} %shard_map.116), channel_id=1, source_target_pairs={{0,2},{2,0},{4,6},{6,4},{8,10},{10,8},{12,14},{14,12},{1,3},{3,1},... | collective-permute-start | bytes 1572872 | tf_op jit(solution)/shard_map/ppermute | solution.py:400
  24.2 4.3 %shard_map.117 = (f32[4,1024,128]{2,1,0:T(8,128)S(1)}, f32[4,1024,256]{2,1,0:T(8,128)S(1)}, bf16[256,512]{1,0:T(8,128)(2,1)}, bf16[256,512]{1,0:T(8,128)(2,1)}) custom-call(bf16[128,4096]{1,0:T(8,128)(2,1)S(1)} %get-tuple-element.47.refs_0_, ...), custom_call_target="tpu_custom_call", output_to_operand_aliasing={{0}: (5, {}), {1}: (6, {}), {2}: (7, {}), {3}: (8, {})} | custom-call | flops 1073741824 | bytes 4194304 | tf_op jit(solution)/shard_map/pallas_call | solution.py:303
  28.5 0.0 collective-permute-done.between
  28.5 5.1 %collective-permute-done.2.refs_0_.at_ends = bf16[512,512]{1,0:T(8,128)(2,1)S(1)} collective-permute-done((bf16[512,512]{1,0:T(8,128)(2,1)S(1)}, bf16[512,512]{1,0:T(8,128)(2,1)S(1)}, u32[]{:S(2)}, u32[]{:S(2)}) %collective-permute-start.2) | collective-permute-done | bytes 524320 | tf_op jit(solution)/shard_map/ppermute | solution.py:400
  33.7 0.1 collective-permute-start.4
  33.7 1.4 %collective-permute-done.5.refs_0_.refs_4_ = bf16[512,512]{1,0:T(8,128)(2,1)S(1)} collective-permute-done((bf16[512,512]{1,0:T(8,128)(2,1)S(1)}, bf16[512,512]{1,0:T(8,128)(2,1)S(1)}, u32[]{:S(2)}, u32[]{:S(2)}) %collective-permute-start.5) | collective-permute-done | bytes 524320 | tf_op jit(solution)/shard_map/ppermute | solution.py:400
  35.2 0.2 shard_map.118.refs_3_
  35.4 1.6 %collective-permute-start.7 = (bf16[512,512]{1,0:T(8,128)(2,1)S(1)}, bf16[512,512]{1,0:T(8,128)(2,1)S(1)}, u32[]{:S(2)}, u32[]{:S(2)}) collective-permute-start(bf16[512,512]{1,0:T(8,128)(2,1)S(1)} %shard_map.118.refs_3_), channel_id=1, source_target_pairs={{0,2},{2,0},{4,6},{6,4},{8,10},{10,8},{12,14},{14,12},{1,3},{3,1},... | collective-permute-start | bytes 1572872 | tf_op jit(solution)/shard_map/ppermute | solution.py:400
  37.0 4.3 %shard_map.119 = (f32[4,1024,128]{2,1,0:T(8,128)S(1)}, f32[4,1024,256]{2,1,0:T(8,128)S(1)}, bf16[256,512]{1,0:T(8,128)(2,1)}, bf16[256,512]{1,0:T(8,128)(2,1)}) custom-call(bf16[128,4096]{1,0:T(8,128)(2,1)S(1)} %get-tuple-element.47.refs_0_, ...), custom_call_target="tpu_custom_call", output_to_operand_aliasing={{0}: (5, {}), {1}: (6, {}), {2}: (7, {}), {3}: (8, {})} | custom-call | flops 1073741824 | bytes 4194304 | tf_op jit(solution)/shard_map/pallas_call | solution.py:303
  41.3 4.6 %collective-permute-done.4.in_ref.refs_3_ = bf16[512,512]{1,0:T(8,128)(2,1)S(1)} collective-permute-done((bf16[512,512]{1,0:T(8,128)(2,1)S(1)}, bf16[512,512]{1,0:T(8,128)(2,1)S(1)}, u32[]{:S(2)}, u32[]{:S(2)}) %collective-permute-start.4) | collective-permute-done | bytes 524320 | tf_op jit(solution)/shard_map/ppermute | solution.py:400
  45.9 1.2 %collective-permute-start.6 = (bf16[256,512]{1,0:T(8,128)(2,1)S(1)}, bf16[256,512]{1,0:T(8,128)(2,1)S(1)}, u32[]{:S(2)}, u32[]{:S(2)}) collective-permute-start(bf16[256,512]{1,0:T(8,128)(2,1)S(1)} %shard_map.120.refs_0_), channel_id=1, source_target_pairs={{0,2},{2,0},{4,6},{6,4},{8,10},{10,8},{12,14},{14,12},{1,3},{3,1},... | collective-permute-start | bytes 786440 | tf_op jit(solution)/shard_map/ppermute | solution.py:400
  47.2 0.8 %collective-permute-done.7.in_ref.refs_4_ = bf16[512,512]{1,0:T(8,128)(2,1)S(1)} collective-permute-done((bf16[512,512]{1,0:T(8,128)(2,1)S(1)}, bf16[512,512]{1,0:T(8,128)(2,1)S(1)}, u32[]{:S(2)}, u32[]{:S(2)}) %collective-permute-start.7) | collective-permute-done | bytes 524320 | tf_op jit(solution)/shard_map/ppermute | solution.py:400
  48.0 1.6 %collective-permute-start.8 = (bf16[256,512]{1,0:T(8,128)(2,1)S(1)}, bf16[256,512]{1,0:T(8,128)(2,1)S(1)}, u32[]{:S(2)}, u32[]{:S(2)}) collective-permute-start(bf16[256,512]{1,0:T(8,128)(2,1)S(1)} %shard_map.122), channel_id=1, source_target_pairs={{0,4},{2,6},{4,0},{6,2},{8,12},{10,14},{12,8},{14,10},{1,5},{3,7},... | collective-permute-start | bytes 786440 | tf_op jit(solution)/shard_map/ppermute | solution.py:400
  49.6 4.3 %shard_map.123 = (f32[4,1024,128]{2,1,0:T(8,128)S(1)}, f32[4,1024,256]{2,1,0:T(8,128)S(1)}, bf16[256,512]{1,0:T(8,128)(2,1)}, bf16[256,512]{1,0:T(8,128)(2,1)}) custom-call(bf16[128,4096]{1,0:T(8,128)(2,1)S(1)} %get-tuple-element.47.refs_0_, ...), custom_call_target="tpu_custom_call", output_to_operand_aliasing={{0}: (5, {}), {1}: (6, {}), {2}: (7, {}), {3}: (8, {})} | custom-call | flops 1073741824 | bytes 4194304 | tf_op jit(solution)/shard_map/pallas_call | solution.py:303
  53.9 0.0 collective-permute-done.6.at_ends.between
  54.0 0.5 collective-permute-done.8.refs_4_
  54.4 2.6 %shard_map.124 = (bf16[128,4096]{1,0:T(8,128)(2,1)}, bf16[256,512]{1,0:T(8,128)(2,1)}, bf16[256,512]{1,0:T(8,128)(2,1)}) custom-call(bf16[128,4096]{1,0:T(8,128)(2,1)S(1)} %get-tuple-element.47.refs_0_, f32[8,128,256]{2,1,0:T(8,128)S(1)} %get-tuple-element.48.refs_1_, ...), custom_call_target="tpu_custom_call", output_to_operand_aliasing={{1}: (7, {}), {2}: (8, {})} | custom-call | flops 536870912 | bytes 4194304 | tf_op jit(solution)/shard_map/pallas_call | solution.py:303
  (5 shorter events, 0.1 us)
Async XLA Ops:
  1.8 15.0 %collective-permute-start.1 = (bf16[512,512]{1,0:T(8,128)(2,1)S(1)}, bf16[512,512]{1,0:T(8,128)(2,1)S(1)}, u32[]{:S(2)}, u32[]{:S(2)}) collective-permute-start(bf16[512,512]{1,0:T(8,128)(2,1)S(1)} %shard_map.112.own_ref.at_ends.between), channel_id=1, source_target_pairs={{0,4},{2,6},{4,0},{6,2},{8,12},{10,14},{12,8},{14,10},{1,5},{3,7},... | collective-permute-start | bytes 1572872 | tf_op jit(solution)/shard_map/ppermute | solution.py:400
  4.9 17.7 %collective-permute-start.3 = (bf16[512,512]{1,0:T(8,128)(2,1)S(1)}, bf16[512,512]{1,0:T(8,128)(2,1)S(1)}, u32[]{:S(2)}, u32[]{:S(2)}) collective-permute-start(bf16[512,512]{1,0:T(8,128)(2,1)S(1)} %shard_map.112.own_ref.at_ends.between), channel_id=1, source_target_pairs={{0,2},{2,0},{4,6},{6,4},{8,10},{10,8},{12,14},{14,12},{1,3},{3,1},... | collective-permute-start | bytes 1572872 | tf_op jit(solution)/shard_map/ppermute | solution.py:400
  6.4 22.1 %collective-permute-start = (bf16[512,512]{1,0:T(8,128)(2,1)S(1)}, bf16[512,512]{1,0:T(8,128)(2,1)S(1)}, u32[]{:S(2)}, u32[]{:S(2)}) collective-permute-start(bf16[512,512]{1,0:T(8,128)(2,1)S(1)} %shard_map.112.own_ref.at_ends.between), channel_id=1, source_target_pairs={{4,8},{6,10},{8,4},{10,6},{5,9},{7,11},{9,5},{11,7},{20,24},{22,26... | collective-permute-start | bytes 1572872 | tf_op jit(solution)/shard_map/ppermute | solution.py:400
  16.8 16.8 %collective-permute-start.2 = (bf16[512,512]{1,0:T(8,128)(2,1)S(1)}, bf16[512,512]{1,0:T(8,128)(2,1)S(1)}, u32[]{:S(2)}, u32[]{:S(2)}) collective-permute-start(bf16[512,512]{1,0:T(8,128)(2,1)S(1)} %shard_map.114.refs_1_), channel_id=1, source_target_pairs={{0,12},{2,14},{12,0},{14,2},{1,13},{3,15},{13,1},{15,3},{16,28},{1... | collective-permute-start | bytes 1572872 | tf_op jit(solution)/shard_map/ppermute | solution.py:400
  22.6 12.6 %collective-permute-start.5 = (bf16[512,512]{1,0:T(8,128)(2,1)S(1)}, bf16[512,512]{1,0:T(8,128)(2,1)S(1)}, u32[]{:S(2)}, u32[]{:S(2)}) collective-permute-start(bf16[512,512]{1,0:T(8,128)(2,1)S(1)} %shard_map.116), channel_id=1, source_target_pairs={{0,2},{2,0},{4,6},{6,4},{8,10},{10,8},{12,14},{14,12},{1,3},{3,1},... | collective-permute-start | bytes 1572872 | tf_op jit(solution)/shard_map/ppermute | solution.py:400
  33.7 12.2 %collective-permute-start.4 = (bf16[512,512]{1,0:T(8,128)(2,1)S(1)}, bf16[512,512]{1,0:T(8,128)(2,1)S(1)}, u32[]{:S(2)}, u32[]{:S(2)}) collective-permute-start(bf16[512,512]{1,0:T(8,128)(2,1)S(1)} %shard_map.115), channel_id=1, source_target_pairs={{0,8},{2,10},{12,4},{14,6},{8,12},{10,14},{4,0},{6,2},{1,9},{3,11}... | collective-permute-start | bytes 1572872 | tf_op jit(solution)/shard_map/ppermute | solution.py:400
  35.4 12.6 %collective-permute-start.7 = (bf16[512,512]{1,0:T(8,128)(2,1)S(1)}, bf16[512,512]{1,0:T(8,128)(2,1)S(1)}, u32[]{:S(2)}, u32[]{:S(2)}) collective-permute-start(bf16[512,512]{1,0:T(8,128)(2,1)S(1)} %shard_map.118.refs_3_), channel_id=1, source_target_pairs={{0,2},{2,0},{4,6},{6,4},{8,10},{10,8},{12,14},{14,12},{1,3},{3,1},... | collective-permute-start | bytes 1572872 | tf_op jit(solution)/shard_map/ppermute | solution.py:400
  45.9 8.0 %collective-permute-start.6 = (bf16[256,512]{1,0:T(8,128)(2,1)S(1)}, bf16[256,512]{1,0:T(8,128)(2,1)S(1)}, u32[]{:S(2)}, u32[]{:S(2)}) collective-permute-start(bf16[256,512]{1,0:T(8,128)(2,1)S(1)} %shard_map.120.refs_0_), channel_id=1, source_target_pairs={{0,2},{2,0},{4,6},{6,4},{8,10},{10,8},{12,14},{14,12},{1,3},{3,1},... | collective-permute-start | bytes 786440 | tf_op jit(solution)/shard_map/ppermute | solution.py:400
  48.0 6.4 %collective-permute-start.8 = (bf16[256,512]{1,0:T(8,128)(2,1)S(1)}, bf16[256,512]{1,0:T(8,128)(2,1)S(1)}, u32[]{:S(2)}, u32[]{:S(2)}) collective-permute-start(bf16[256,512]{1,0:T(8,128)(2,1)S(1)} %shard_map.122), channel_id=1, source_target_pairs={{0,4},{2,6},{4,0},{6,2},{8,12},{10,14},{12,8},{14,10},{1,5},{3,7},... | collective-permute-start | bytes 786440 | tf_op jit(solution)/shard_map/ppermute | solution.py:400

commit v6 on v5

--- a/solution.py
+++ b/solution.py
@@ -28,10 +28,13 @@
 
 
 def part_of(block, which, rows, start, size):
-    if len(block) == 1:
-        return block[0][which * rows:(which + 1) * rows, start:start + size]
-    half, inner = divmod(which, 2)
-    return block[half][inner * rows:(inner + 1) * rows, start:start + size]
+    first, stop, found = which * rows, (which + 1) * rows, []
+    for part in block:
+        length = part.shape[0]
+        if first < min(stop, length):
+            found.append(part[first:min(stop, length), start:start + size])
+        first, stop = max(first - length, 0), stop - length
+    return found[0] if len(found) == 1 else jnp.concatenate(found, axis=0)
 
 
 def add_blocks(blocks, biases, query_ref, before, after, heads, groups, store):
@@ -361,17 +364,16 @@
     )(in_vmem(at_ends), in_vmem(between), *(in_vmem(x) for x in after))
 
 
-def half_kernel(which, in_ref, *refs):
+def rows_kernel(first, in_ref, *refs):
     out_ref = refs[-1]
-    rows = out_ref.shape[0]
-    out_ref[...] = in_ref[which * rows:(which + 1) * rows]
-
-
-def half_of(x, which, *after):
+    out_ref[...] = in_ref[first:first + out_ref.shape[0]]
+
+
+def rows_of(x, first, stop, *after):
     vmem = pl.BlockSpec(memory_space=VMEM)
     return pl.pallas_call(
-        functools.partial(half_kernel, which),
-        out_shape=VMEM((x.shape[0] // 2, x.shape[1]), x.dtype),
+        functools.partial(rows_kernel, first),
+        out_shape=VMEM((stop - first, x.shape[1]), x.dtype),
         in_specs=[vmem] * (1 + len(after)),
         out_specs=vmem,
         compiler_params=pltpu.CompilerParams(vmem_limit_bytes=8 * 1024 * 1024),
@@ -401,7 +403,7 @@
 
     small = (placement, span_lens, prefix_lens, decode_dest.reshape(cycle, rows))
     own = pack(prefix_keys, prefix_values, new_keys, new_values)
-    half = own.shape[0] // 2
+    cut = own.shape[0] * 9 // 32 * 2
 
     offsets = (0, 2, 1, 6, 3, 4, 7, 5)
 
@@ -423,9 +425,9 @@
     y_b = send(b, swap)
     carry = run_stage(common, (3, 4), offsets[3:5], [[b], [y_a]], carry, False)
 
-    c_low = half_of(c, 0, carry[0])
+    c_low = rows_of(c, 0, cut, carry[0])
     y_c_low = send(c_low, swap)
-    y_b_high, *carry = together((half_of(y_b, 1, c_low), *carry))
+    y_b_high, *carry = together((rows_of(y_b, cut, y_b.shape[0], c_low), *carry))
     y_c_high = send(y_b_high, near)
     carry = run_stage(common, (5, 6), offsets[5:7], [[c], [y_b]], carry, False)
     return tuple(run_stage(common, (7,), offsets[7:], [[choose(y_c_low, y_c_low), y_c_high]], carry, True))

time: 57.4 us -> 57 us (level)
  transfers between devices with their start and end apart: 9 -> 9, of which waited for: 6 -> 6; matrix products, arithmetic and copies ran while one was open for 0% -> 0% of each run, Pallas kernels for 29% -> 30%
where the time goes in v6:
time: 57 us; the launch traced here: 56.8 us
  Pallas kernels  20.6 us (36%)
  waiting for transfers between devices  18.3 us (32%)
  starting transfers between devices  17 us (30%)
  between operations  0.93 us (2%)
    ppermute x9, waiting for transfers between devices, cycle_of_eight(): send = lambda x, table: lax.ppermute(x, 'blk', table)  18.3 us
    ppermute x9, starting transfers between devices, cycle_of_eight(): send = lambda x, table: lax.ppermute(x, 'blk', table)  17 us
    pallas_call x4, Pallas kernels, run_stage(): pl.pallas_call(functools.partial(stage_kernel, order, offsets, parts, las...  15.6 us
    pallas_call x1, Pallas kernels, run_first(): pl.pallas_call(functools.partial(first_kernel, offsets, rows, heads, grou...  3.41 us
  transfers between devices with their start and end apart: 9, of which 6 were waited for; matrix products, arithmetic and copies ran while one was open for 0% of the time, Pallas kernels for 30%

profile of v6, /device:TPU:0, one launch (start us, length us, event | category | flops | bytes accessed | tf_op | source)
XLA Modules:
  0.0 56.8 jit_solution(325327813161075061)
XLA Ops:
  0.6 1.1 %shard_map.112.own_ref.at_ends.between = bf16[512,512]{1,0:T(8,128)(2,1)S(1)} custom-call(bf16[128,512]{1,0:T(8,128)(2,1)} %refs_0_.1, bf16[128,512]{1,0:T(8,128)(2,1)} %refs_1_.1, bf16[128,512]{1,0:T(8,128)(2,1)} %refs_2_.1, bf16[128,512]{1,0:T(8,128)(2,1)} %refs_3_.1), custom_call_target="tpu_custom_call" | custom-call | tf_op jit(solution)/shard_map/pallas_call | solution.py:332
  1.8 3.1 %collective-permute-start.1 = (bf16[512,512]{1,0:T(8,128)(2,1)S(1)}, bf16[512,512]{1,0:T(8,128)(2,1)S(1)}, u32[]{:S(2)}, u32[]{:S(2)}) collective-permute-start(bf16[512,512]{1,0:T(8,128)(2,1)S(1)} %shard_map.112.own_ref.at_ends.between), channel_id=1, source_target_pairs={{0,4},{2,6},{4,0},{6,2},{8,12},{10,14},{12,8},{14,10},{1,5},{3,7},... | collective-permute-start | bytes 1572872 | tf_op jit(solution)/shard_map/ppermute | solution.py:402
  4.9 1.5 %collective-permute-start.3 = (bf16[512,512]{1,0:T(8,128)(2,1)S(1)}, bf16[512,512]{1,0:T(8,128)(2,1)S(1)}, u32[]{:S(2)}, u32[]{:S(2)}) collective-permute-start(bf16[512,512]{1,0:T(8,128)(2,1)S(1)} %shard_map.112.own_ref.at_ends.between), channel_id=1, source_target_pairs={{0,2},{2,0},{4,6},{6,4},{8,10},{10,8},{12,14},{14,12},{1,3},{3,1},... | collective-permute-start | bytes 1572872 | tf_op jit(solution)/shard_map/ppermute | solution.py:402
  6.4 0.7 %collective-permute-start = (bf16[512,512]{1,0:T(8,128)(2,1)S(1)}, bf16[512,512]{1,0:T(8,128)(2,1)S(1)}, u32[]{:S(2)}, u32[]{:S(2)}) collective-permute-start(bf16[512,512]{1,0:T(8,128)(2,1)S(1)} %shard_map.112.own_ref.at_ends.between), channel_id=1, source_target_pairs={{4,8},{6,10},{8,4},{10,6},{5,9},{7,11},{9,5},{11,7},{20,24},{22,26... | collective-permute-start | bytes 1572872 | tf_op jit(solution)/shard_map/ppermute | solution.py:402
  7.1 3.4 %shard_map.113 = (f32[4,1024,128]{2,1,0:T(8,128)S(1)}, f32[4,1024,256]{2,1,0:T(8,128)S(1)}, bf16[256,512]{1,0:T(8,128)(2,1)}, bf16[256,512]{1,0:T(8,128)(2,1)}, ...) custom-call(s32[1024]{0:T(1024)} %place_in.1, s32[2]{0:T(128)} %span_in.1, ...), custom_call_target="tpu_custom_call" | custom-call | flops 536870912 | bytes 4194304 | tf_op jit(solution)/shard_map/pallas_call | solution.py:258
  10.5 6.3 %collective-permute-done.1.refs_0_.at_ends.between.refs_3_ = bf16[512,512]{1,0:T(8,128)(2,1)S(1)} collective-permute-done((bf16[512,512]{1,0:T(8,128)(2,1)S(1)}, bf16[512,512]{1,0:T(8,128)(2,1)S(1)}, u32[]{:S(2)}, u32[]{:S(2)}) %collective-permute-start.1) | collective-permute-done | bytes 524320 | tf_op jit(solution)/shard_map/ppermute | solution.py:402
  16.8 5.7 %collective-permute-start.2 = (bf16[512,512]{1,0:T(8,128)(2,1)S(1)}, bf16[512,512]{1,0:T(8,128)(2,1)S(1)}, u32[]{:S(2)}, u32[]{:S(2)}) collective-permute-start(bf16[512,512]{1,0:T(8,128)(2,1)S(1)} %shard_map.114.refs_1_), channel_id=1, source_target_pairs={{0,12},{2,14},{12,0},{14,2},{1,13},{3,15},{13,1},{15,3},{16,28},{1... | collective-permute-start | bytes 1572872 | tf_op jit(solution)/shard_map/ppermute | solution.py:402
  22.5 0.0 collective-permute-done.3.refs_0_.refs_4_
  22.5 0.1 shard_map.116
  22.6 1.6 %collective-permute-start.5 = (bf16[512,512]{1,0:T(8,128)(2,1)S(1)}, bf16[512,512]{1,0:T(8,128)(2,1)S(1)}, u32[]{:S(2)}, u32[]{:S(2)}) collective-permute-start(bf16[512,512]{1,0:T(8,128)(2,1)S(1)} %shard_map.116), channel_id=1, source_target_pairs={{0,2},{2,0},{4,6},{6,4},{8,10},{10,8},{12,14},{14,12},{1,3},{3,1},... | collective-permute-start | bytes 1572872 | tf_op jit(solution)/shard_map/ppermute | solution.py:402
  24.2 4.3 %shard_map.117 = (f32[4,1024,128]{2,1,0:T(8,128)S(1)}, f32[4,1024,256]{2,1,0:T(8,128)S(1)}, bf16[256,512]{1,0:T(8,128)(2,1)}, bf16[256,512]{1,0:T(8,128)(2,1)}) custom-call(bf16[128,4096]{1,0:T(8,128)(2,1)S(1)} %get-tuple-element.47.refs_0_, ...), custom_call_target="tpu_custom_call", output_to_operand_aliasing={{0}: (5, {}), {1}: (6, {}), {2}: (7, {}), {3}: (8, {})} | custom-call | flops 1073741824 | bytes 4194304 | tf_op jit(solution)/shard_map/pallas_call | solution.py:306
  28.5 0.0 collective-permute-done.between
  28.5 5.1 %collective-permute-done.2.refs_0_.at_ends = bf16[512,512]{1,0:T(8,128)(2,1)S(1)} collective-permute-done((bf16[512,512]{1,0:T(8,128)(2,1)S(1)}, bf16[512,512]{1,0:T(8,128)(2,1)S(1)}, u32[]{:S(2)}, u32[]{:S(2)}) %collective-permute-start.2) | collective-permute-done | bytes 524320 | tf_op jit(solution)/shard_map/ppermute | solution.py:402
  33.7 0.1 collective-permute-start.4
  33.7 1.4 %collective-permute-done.5.refs_0_.refs_4_ = bf16[512,512]{1,0:T(8,128)(2,1)S(1)} collective-permute-done((bf16[512,512]{1,0:T(8,128)(2,1)S(1)}, bf16[512,512]{1,0:T(8,128)(2,1)S(1)}, u32[]{:S(2)}, u32[]{:S(2)}) %collective-permute-start.5) | collective-permute-done | bytes 524320 | tf_op jit(solution)/shard_map/ppermute | solution.py:402
  35.2 0.2 shard_map.118.refs_3_
  35.4 1.6 %collective-permute-start.7 = (bf16[512,512]{1,0:T(8,128)(2,1)S(1)}, bf16[512,512]{1,0:T(8,128)(2,1)S(1)}, u32[]{:S(2)}, u32[]{:S(2)}) collective-permute-start(bf16[512,512]{1,0:T(8,128)(2,1)S(1)} %shard_map.118.refs_3_), channel_id=1, source_target_pairs={{0,2},{2,0},{4,6},{6,4},{8,10},{10,8},{12,14},{14,12},{1,3},{3,1},... | collective-permute-start | bytes 1572872 | tf_op jit(solution)/shard_map/ppermute | solution.py:402
  37.0 4.3 %shard_map.119 = (f32[4,1024,128]{2,1,0:T(8,128)S(1)}, f32[4,1024,256]{2,1,0:T(8,128)S(1)}, bf16[256,512]{1,0:T(8,128)(2,1)}, bf16[256,512]{1,0:T(8,128)(2,1)}) custom-call(bf16[128,4096]{1,0:T(8,128)(2,1)S(1)} %get-tuple-element.47.refs_0_, ...), custom_call_target="tpu_custom_call", output_to_operand_aliasing={{0}: (5, {}), {1}: (6, {}), {2}: (7, {}), {3}: (8, {})} | custom-call | flops 1073741824 | bytes 4194304 | tf_op jit(solution)/shard_map/pallas_call | solution.py:306
  41.3 4.6 %collective-permute-done.4.in_ref.refs_3_ = bf16[512,512]{1,0:T(8,128)(2,1)S(1)} collective-permute-done((bf16[512,512]{1,0:T(8,128)(2,1)S(1)}, bf16[512,512]{1,0:T(8,128)(2,1)S(1)}, u32[]{:S(2)}, u32[]{:S(2)}) %collective-permute-start.4) | collective-permute-done | bytes 524320 | tf_op jit(solution)/shard_map/ppermute | solution.py:402
  45.9 1.2 %collective-permute-start.6 = (bf16[288,512]{1,0:T(8,128)(2,1)S(1)}, bf16[288,512]{1,0:T(8,128)(2,1)S(1)}, u32[]{:S(2)}, u32[]{:S(2)}) collective-permute-start(bf16[288,512]{1,0:T(8,128)(2,1)S(1)} %shard_map.120.refs_0_), channel_id=1, source_target_pairs={{0,2},{2,0},{4,6},{6,4},{8,10},{10,8},{12,14},{14,12},{1,3},{3,1},... | collective-permute-start | bytes 884744 | tf_op jit(solution)/shard_map/ppermute | solution.py:402
  47.2 0.8 %collective-permute-done.7.in_ref.refs_4_ = bf16[512,512]{1,0:T(8,128)(2,1)S(1)} collective-permute-done((bf16[512,512]{1,0:T(8,128)(2,1)S(1)}, bf16[512,512]{1,0:T(8,128)(2,1)S(1)}, u32[]{:S(2)}, u32[]{:S(2)}) %collective-permute-start.7) | collective-permute-done | bytes 524320 | tf_op jit(solution)/shard_map/ppermute | solution.py:402
  48.0 1.6 %collective-permute-start.8 = (bf16[224,512]{1,0:T(8,128)(2,1)S(1)}, bf16[224,512]{1,0:T(8,128)(2,1)S(1)}, u32[]{:S(2)}, u32[]{:S(2)}) collective-permute-start(bf16[224,512]{1,0:T(8,128)(2,1)S(1)} %shard_map.122), channel_id=1, source_target_pairs={{0,4},{2,6},{4,0},{6,2},{8,12},{10,14},{12,8},{14,10},{1,5},{3,7},... | collective-permute-start | bytes 688136 | tf_op jit(solution)/shard_map/ppermute | solution.py:402
  49.6 4.3 %shard_map.123 = (f32[4,1024,128]{2,1,0:T(8,128)S(1)}, f32[4,1024,256]{2,1,0:T(8,128)S(1)}, bf16[256,512]{1,0:T(8,128)(2,1)}, bf16[256,512]{1,0:T(8,128)(2,1)}) custom-call(bf16[128,4096]{1,0:T(8,128)(2,1)S(1)} %get-tuple-element.47.refs_0_, ...), custom_call_target="tpu_custom_call", output_to_operand_aliasing={{0}: (5, {}), {1}: (6, {}), {2}: (7, {}), {3}: (8, {})} | custom-call | flops 1073741824 | bytes 4194304 | tf_op jit(solution)/shard_map/pallas_call | solution.py:306
  53.9 0.0 collective-permute-done.6.at_ends.between
  54.0 0.1 collective-permute-done.8.refs_4_
  54.1 2.6 %shard_map.124 = (bf16[128,4096]{1,0:T(8,128)(2,1)}, bf16[256,512]{1,0:T(8,128)(2,1)}, bf16[256,512]{1,0:T(8,128)(2,1)}) custom-call(bf16[128,4096]{1,0:T(8,128)(2,1)S(1)} %get-tuple-element.47.refs_0_, f32[8,128,256]{2,1,0:T(8,128)S(1)} %get-tuple-element.48.refs_1_, ...), custom_call_target="tpu_custom_call", output_to_operand_aliasing={{1}: (7, {}), {2}: (8, {})} | custom-call | flops 536870912 | bytes 4194304 | tf_op jit(solution)/shard_map/pallas_call | solution.py:306
  (5 shorter events, 0.1 us)
Async XLA Ops:
  1.8 15.0 %collective-permute-start.1 = (bf16[512,512]{1,0:T(8,128)(2,1)S(1)}, bf16[512,512]{1,0:T(8,128)(2,1)S(1)}, u32[]{:S(2)}, u32[]{:S(2)}) collective-permute-start(bf16[512,512]{1,0:T(8,128)(2,1)S(1)} %shard_map.112.own_ref.at_ends.between), channel_id=1, source_target_pairs={{0,4},{2,6},{4,0},{6,2},{8,12},{10,14},{12,8},{14,10},{1,5},{3,7},... | collective-permute-start | bytes 1572872 | tf_op jit(solution)/shard_map/ppermute | solution.py:402
  4.9 17.7 %collective-permute-start.3 = (bf16[512,512]{1,0:T(8,128)(2,1)S(1)}, bf16[512,512]{1,0:T(8,128)(2,1)S(1)}, u32[]{:S(2)}, u32[]{:S(2)}) collective-permute-start(bf16[512,512]{1,0:T(8,128)(2,1)S(1)} %shard_map.112.own_ref.at_ends.between), channel_id=1, source_target_pairs={{0,2},{2,0},{4,6},{6,4},{8,10},{10,8},{12,14},{14,12},{1,3},{3,1},... | collective-permute-start | bytes 1572872 | tf_op jit(solution)/shard_map/ppermute | solution.py:402
  6.4 22.1 %collective-permute-start = (bf16[512,512]{1,0:T(8,128)(2,1)S(1)}, bf16[512,512]{1,0:T(8,128)(2,1)S(1)}, u32[]{:S(2)}, u32[]{:S(2)}) collective-permute-start(bf16[512,512]{1,0:T(8,128)(2,1)S(1)} %shard_map.112.own_ref.at_ends.between), channel_id=1, source_target_pairs={{4,8},{6,10},{8,4},{10,6},{5,9},{7,11},{9,5},{11,7},{20,24},{22,26... | collective-permute-start | bytes 1572872 | tf_op jit(solution)/shard_map/ppermute | solution.py:402
  16.8 16.8 %collective-permute-start.2 = (bf16[512,512]{1,0:T(8,128)(2,1)S(1)}, bf16[512,512]{1,0:T(8,128)(2,1)S(1)}, u32[]{:S(2)}, u32[]{:S(2)}) collective-permute-start(bf16[512,512]{1,0:T(8,128)(2,1)S(1)} %shard_map.114.refs_1_), channel_id=1, source_target_pairs={{0,12},{2,14},{12,0},{14,2},{1,13},{3,15},{13,1},{15,3},{16,28},{1... | collective-permute-start | bytes 1572872 | tf_op jit(solution)/shard_map/ppermute | solution.py:402
  22.6 12.6 %collective-permute-start.5 = (bf16[512,512]{1,0:T(8,128)(2,1)S(1)}, bf16[512,512]{1,0:T(8,128)(2,1)S(1)}, u32[]{:S(2)}, u32[]{:S(2)}) collective-permute-start(bf16[512,512]{1,0:T(8,128)(2,1)S(1)} %shard_map.116), channel_id=1, source_target_pairs={{0,2},{2,0},{4,6},{6,4},{8,10},{10,8},{12,14},{14,12},{1,3},{3,1},... | collective-permute-start | bytes 1572872 | tf_op jit(solution)/shard_map/ppermute | solution.py:402
  33.7 12.2 %collective-permute-start.4 = (bf16[512,512]{1,0:T(8,128)(2,1)S(1)}, bf16[512,512]{1,0:T(8,128)(2,1)S(1)}, u32[]{:S(2)}, u32[]{:S(2)}) collective-permute-start(bf16[512,512]{1,0:T(8,128)(2,1)S(1)} %shard_map.115), channel_id=1, source_target_pairs={{0,8},{2,10},{12,4},{14,6},{8,12},{10,14},{4,0},{6,2},{1,9},{3,11}... | collective-permute-start | bytes 1572872 | tf_op jit(solution)/shard_map/ppermute | solution.py:402
  35.4 12.6 %collective-permute-start.7 = (bf16[512,512]{1,0:T(8,128)(2,1)S(1)}, bf16[512,512]{1,0:T(8,128)(2,1)S(1)}, u32[]{:S(2)}, u32[]{:S(2)}) collective-permute-start(bf16[512,512]{1,0:T(8,128)(2,1)S(1)} %shard_map.118.refs_3_), channel_id=1, source_target_pairs={{0,2},{2,0},{4,6},{6,4},{8,10},{10,8},{12,14},{14,12},{1,3},{3,1},... | collective-permute-start | bytes 1572872 | tf_op jit(solution)/shard_map/ppermute | solution.py:402
  45.9 8.0 %collective-permute-start.6 = (bf16[288,512]{1,0:T(8,128)(2,1)S(1)}, bf16[288,512]{1,0:T(8,128)(2,1)S(1)}, u32[]{:S(2)}, u32[]{:S(2)}) collective-permute-start(bf16[288,512]{1,0:T(8,128)(2,1)S(1)} %shard_map.120.refs_0_), channel_id=1, source_target_pairs={{0,2},{2,0},{4,6},{6,4},{8,10},{10,8},{12,14},{14,12},{1,3},{3,1},... | collective-permute-start | bytes 884744 | tf_op jit(solution)/shard_map/ppermute | solution.py:402
  48.0 6.1 %collective-permute-start.8 = (bf16[224,512]{1,0:T(8,128)(2,1)S(1)}, bf16[224,512]{1,0:T(8,128)(2,1)S(1)}, u32[]{:S(2)}, u32[]{:S(2)}) collective-permute-start(bf16[224,512]{1,0:T(8,128)(2,1)S(1)} %shard_map.122), channel_id=1, source_target_pairs={{0,4},{2,6},{4,0},{6,2},{8,12},{10,14},{12,8},{14,10},{1,5},{3,7},... | collective-permute-start | bytes 688136 | tf_op jit(solution)/shard_map/ppermute | solution.py:402
